TPU v7x, 32 devices: a whole 2x2x4 slice. The times are simulated.
32 devices in a mesh: wide: 8 (over z, y), narrow: 4 (over x, core).
Axes of the slice: x: 2, y: 2, z: 4, core: 2. Of those that a mesh axis runs over, the one named last changes fastest.
Arguments:
- main_residual: bfloat16 [32768, 512], P(('wide', 'narrow')), may hold values from -6 to 6
- side_residual: bfloat16 [32768, 512], P(('wide', 'narrow')), may hold values from -6 to 6
- cotangent: bfloat16 [32768, 512], P(('wide', 'narrow')), may hold values from -6 to 6
- lengths: int32 [32, 4], P(('wide', 'narrow')), may hold values from 0 to 1024, as said below
- input_weight: bfloat16 [2, 512, 1536], P(None, ('wide', 'narrow')), may hold values from -0.375 to 0.375
- output_weight: bfloat16 [2, 512, 512], P(None, ('wide', 'narrow')), may hold values from -0.5 to 0.5
- expand_weight: bfloat16 [2, 512, 2048], P(None, ('wide', 'narrow')), may hold values from -0.25 to 0.25
- reduce_weight: bfloat16 [2, 2048, 512], P(None, ('wide', 'narrow')), may hold values from -0.1875 to 0.1875
- vectors: bfloat16 [2, 6144], P(None, ('wide', 'narrow')), may hold values from -0.9 to 1.5
- final_norm: bfloat16 [1024], P(('wide', 'narrow')), may hold values from -0.9 to 1.5
Outputs:
- layer_out: bfloat16 [32768, 512], P(('wide', 'narrow'))
- grad_main: float32 [32768, 512], P(('wide', 'narrow'))
- grad_side: float32 [32768, 512], P(('wide', 'narrow'))
- grad_input_weight: float32 [2, 512, 1536], P(None, ('wide', 'narrow'))
- grad_output_weight: float32 [2, 512, 512], P(None, ('wide', 'narrow'))
- grad_expand: float32 [2, 512, 2048], P(None, ('wide', 'narrow'))
- grad_reduce: float32 [2, 2048, 512], P(None, ('wide', 'narrow'))
- grad_vectors: float32 [2, 6144], P(None, ('wide', 'narrow'))
- grad_final: float32 [1024], P(('wide', 'narrow'))
Inputs may be any that keep to these rules, and one draw needn't show every extreme that they name: Each row is either one sequence, with a length of half of 1024 to 1024 first and three zeros after it, or four sequences with lengths of 1 to 256. Both kinds occur in every draw, and a length of 1024 and one of 256 are reached.
All inputs are finite; a program needn't handle non-finite values.
Results may differ from a plain program's by a relative error of at most 0.024.
Values may be sent and summed in bfloat16 or wider, within the bound.
No kernel may reach another device: no remote copies, remote signals or barrier semaphores. Data moves between devices by JAX's collectives and lax.ppermute only.
A program may use at most 192 MiB of HBM per device.

v0:
```python
import jax
import jax.numpy as jnp
from jax import lax
from jax.sharding import PartitionSpec as P

HEAD_DIM = 64


def layer_norm(values, gain, shift):
    centered = values - jnp.mean(values, axis=-1, keepdims=True)
    variance = jnp.mean(centered * centered, axis=-1, keepdims=True)
    return centered * lax.rsqrt(variance + 1e-05) * gain + shift


def heads_first(matrix, groups, head_count):
    token_count, features = matrix.shape
    shaped = matrix.reshape(groups, token_count // groups, head_count, features // head_count)
    return shaped.transpose(2, 0, 1, 3)


def rows_first(blocks):
    head_count, groups, per_group, head_size = blocks.shape
    return blocks.transpose(1, 2, 0, 3).reshape(groups * per_group, head_count * head_size)


def split_packed(packed, groups, head_count):
    features = packed.shape[1] // 3
    query_h = heads_first(packed[:, :features], groups, head_count)
    key_h = heads_first(packed[:, features : 2 * features], groups, head_count)
    value_h = heads_first(packed[:, 2 * features :], groups, head_count)
    return (query_h, key_h, value_h)


def masked_scores(query_one, key_one, allowed, score_scale):
    scores = (
        jnp.einsum("gqd,gkd->gqk", query_one, key_one, preferred_element_type=jnp.float32)
        * score_scale
    )
    return jnp.where(allowed[:, None, :], scores, -1000000000.0)


def forward_heads(query_h, key_h, value_h, allowed, score_scale):

    def forward_one_head(operands):
        query_one, key_one, value_one = operands
        scores = masked_scores(query_one, key_one, allowed, score_scale)
        row_max = jnp.max(scores, axis=-1, keepdims=True)
        exponent = jnp.exp(scores - row_max)
        row_sum = jnp.sum(exponent, axis=-1, keepdims=True)
        chances = (exponent / row_sum).astype(jnp.bfloat16)
        context = jnp.einsum("gqk,gkd->gqd", chances, value_one, preferred_element_type=jnp.float32)
        return (context, (row_max + jnp.log(row_sum))[..., 0])

    return lax.map(forward_one_head, (query_h, key_h, value_h))


def backward_heads(query_h, key_h, value_h, allowed, score_scale, logs_h, dcontext_h):

    def backward_one_head(operands):
        query_one, key_one, value_one, log_one, dcontext_one = operands
        scores = masked_scores(query_one, key_one, allowed, score_scale)
        chances = jnp.exp(scores - log_one[..., None])
        chances_low = chances.astype(jnp.bfloat16)
        dchances = jnp.einsum(
            "gqd,gkd->gqk", dcontext_one, value_one, preferred_element_type=jnp.float32
        )
        row_dot = jnp.sum(chances * dchances, axis=-1, keepdims=True)
        dscores = (chances * (dchances - row_dot)).astype(jnp.bfloat16)
        dquery = (
            jnp.einsum("gqk,gkd->gqd", dscores, key_one, preferred_element_type=jnp.float32)
            * score_scale
        )
        dkey = (
            jnp.einsum("gqk,gqd->gkd", dscores, query_one, preferred_element_type=jnp.float32)
            * score_scale
        )
        dvalue = jnp.einsum(
            "gqk,gqd->gkd", chances_low, dcontext_one, preferred_element_type=jnp.float32
        )
        return (dquery, dkey, dvalue)

    return lax.map(backward_one_head, (query_h, key_h, value_h, logs_h, dcontext_h))


def slot_forward(packed, bounds, head_count, score_scale):
    positions = packed.shape[0]

    def with_groups(groups):

        def branch_fn(slot_packed, slot_bounds):
            query_h, key_h, value_h = split_packed(slot_packed, groups, head_count)
            allowed = jnp.arange(positions // groups)[None, :] < slot_bounds[:groups, None]
            context, log_sums = forward_heads(query_h, key_h, value_h, allowed, score_scale)
            return (rows_first(context), log_sums.reshape(head_count, positions))

        return branch_fn

    return lax.cond(bounds[1] == 0, with_groups(1), with_groups(4), packed, bounds)


def slot_backward(packed, bounds, log_sums, dcontext, head_count, score_scale):
    positions = packed.shape[0]

    def with_groups(groups):

        def branch_fn(slot_packed, slot_bounds, slot_logs, slot_dcontext):
            query_h, key_h, value_h = split_packed(slot_packed, groups, head_count)
            allowed = jnp.arange(positions // groups)[None, :] < slot_bounds[:groups, None]
            logs_h = slot_logs.reshape(head_count, groups, positions // groups)
            dcontext_h = heads_first(slot_dcontext, groups, head_count)
            dquery, dkey, dvalue = backward_heads(
                query_h, key_h, value_h, allowed, score_scale, logs_h, dcontext_h
            )
            return jnp.concatenate(
                [rows_first(dquery), rows_first(dkey), rows_first(dvalue)], axis=1
            )

        return branch_fn

    return lax.cond(
        bounds[1] == 0, with_groups(1), with_groups(4), packed, bounds, log_sums, dcontext
    )


def local(
    main_residual,
    side_residual,
    cotangent,
    lengths,
    input_weight,
    output_weight,
    expand_weight,
    reduce_weight,
    vectors,
    final_norm,
):
    token_count, features = main_residual.shape
    slot_count = lengths.shape[0]
    positions = token_count // slot_count
    layer_count = input_weight.shape[0]
    head_count = features // HEAD_DIM
    score_scale = HEAD_DIM ** (-0.5)
    all_vectors, final_full = (
        lax.all_gather(vectors, ("wide", "narrow"), axis=1, tiled=True),
        lax.all_gather(final_norm, ("wide", "narrow"), axis=0, tiled=True),
    )
    all_vectors = all_vectors.astype(jnp.float32)
    final_full = final_full.astype(jnp.float32)

    def pieces_of(layer_index):
        layer_vectors = all_vectors[layer_index]
        pieces = [
            layer_vectors[block_index * features : (block_index + 1) * features]
            for block_index in range(8)
        ]
        return (pieces, layer_vectors[8 * features :])

    def packed_of(rounded, in_full, pieces):
        bias_in = jnp.concatenate([pieces[0], jnp.zeros_like(pieces[0]), pieces[1]])
        return (jnp.dot(rounded, in_full, preferred_element_type=jnp.float32) + bias_in).astype(
            jnp.bfloat16
        )

    def ffn_of(main_rows, up_full, down_full, pieces, up_bias):
        rounded = main_rows.astype(jnp.bfloat16)
        hidden = jnp.dot(rounded, up_full, preferred_element_type=jnp.float32) + up_bias
        activated, gelu_back = jax.vjp(jax.nn.gelu, hidden)
        activated = activated.astype(jnp.bfloat16)
        branch = jnp.dot(activated, down_full, preferred_element_type=jnp.float32) + pieces[5]
        return (rounded, activated, gelu_back, branch)

    def slot_view(matrix):
        return matrix.reshape(slot_count, positions, matrix.shape[1])

    main_rows = main_residual.astype(jnp.float32)
    side_rows = side_residual.astype(jnp.float32)
    kept = []
    for layer_index in range(layer_count):
        pieces, up_bias = pieces_of(layer_index)
        attn_pair = (
            lax.all_gather(input_weight[layer_index], ("wide", "narrow"), axis=0, tiled=True),
            lax.all_gather(output_weight[layer_index], ("wide", "narrow"), axis=0, tiled=True),
        )
        in_full, out_full = attn_pair
        packed = packed_of(main_rows.astype(jnp.bfloat16), in_full, pieces)
        context, log_sums = lax.map(
            lambda slot_items: slot_forward(slot_items[0], slot_items[1], head_count, score_scale),
            (slot_view(packed), lengths),
        )
        context = context.reshape(token_count, features).astype(jnp.bfloat16)
        branch = jnp.dot(context, out_full, preferred_element_type=jnp.float32) + pieces[2]
        attn_input = main_rows
        main_rows = layer_norm(main_rows + branch, pieces[3], pieces[4])
        side_rows = side_rows + branch
        ffn_pair = (
            lax.all_gather(expand_weight[layer_index], ("wide", "narrow"), axis=0, tiled=True),
            lax.all_gather(reduce_weight[layer_index], ("wide", "narrow"), axis=0, tiled=True),
        )
        ffn_input = main_rows
        branch = ffn_of(main_rows, ffn_pair[0], ffn_pair[1], pieces, up_bias)[3]
        main_rows = layer_norm(main_rows + branch, pieces[6], pieces[7])
        side_rows = side_rows + branch
        kept.append((attn_input, context, log_sums, ffn_input, attn_pair, ffn_pair))
    normed, final_back = jax.vjp(
        layer_norm, side_rows, final_full[:features], final_full[features:]
    )
    layer_out = (main_rows + normed).astype(jnp.bfloat16)
    grad_main = cotangent.astype(jnp.float32)
    grad_side, grad_gain, grad_shift = final_back(grad_main)
    layer_grads = [None] * layer_count
    for layer_index in reversed(range(layer_count)):
        attn_input, context, log_sums, ffn_input, attn_pair, ffn_pair = kept[layer_index]
        pieces, up_bias = pieces_of(layer_index)
        ffn_pair = (
            lax.all_gather(expand_weight[layer_index], ("wide", "narrow"), axis=0, tiled=True),
            lax.all_gather(reduce_weight[layer_index], ("wide", "narrow"), axis=0, tiled=True),
        )
        up_full, down_full = ffn_pair
        rounded, activated, gelu_back, branch = ffn_of(
            ffn_input, up_full, down_full, pieces, up_bias
        )
        norm_back = jax.vjp(layer_norm, ffn_input + branch, pieces[6], pieces[7])[1]
        dsum, dgain_two, dshift_two = norm_back(grad_main)
        dbranch = (dsum + grad_side).astype(jnp.bfloat16)
        dbias_two = jnp.sum(dbranch.astype(jnp.float32), axis=0)
        dreduce = jnp.einsum("tf,td->fd", activated, dbranch, preferred_element_type=jnp.float32)
        dactivated = jnp.einsum("td,fd->tf", dbranch, down_full, preferred_element_type=jnp.float32)
        dhidden = gelu_back(dactivated)[0].astype(jnp.bfloat16)
        dbias_up = jnp.sum(dhidden.astype(jnp.float32), axis=0)
        dexpand = jnp.einsum("td,tf->df", rounded, dhidden, preferred_element_type=jnp.float32)
        grad_main = dsum + jnp.einsum(
            "tf,df->td", dhidden, up_full, preferred_element_type=jnp.float32
        )
        attn_pair = (
            lax.all_gather(input_weight[layer_index], ("wide", "narrow"), axis=0, tiled=True),
            lax.all_gather(output_weight[layer_index], ("wide", "narrow"), axis=0, tiled=True),
        )
        in_full, out_full = attn_pair
        branch = jnp.dot(context, out_full, preferred_element_type=jnp.float32) + pieces[2]
        norm_back = jax.vjp(layer_norm, attn_input + branch, pieces[3], pieces[4])[1]
        dsum, dgain_one, dshift_one = norm_back(grad_main)
        dbranch = (dsum + grad_side).astype(jnp.bfloat16)
        dbias_out = jnp.sum(dbranch.astype(jnp.float32), axis=0)
        doutput = jnp.einsum("td,te->de", context, dbranch, preferred_element_type=jnp.float32)
        dcontext = jnp.einsum(
            "te,de->td", dbranch, out_full, preferred_element_type=jnp.float32
        ).astype(jnp.bfloat16)
        rounded = attn_input.astype(jnp.bfloat16)
        packed = packed_of(rounded, in_full, pieces)
        dpacked = lax.map(
            lambda slot_items: slot_backward(
                slot_items[0], slot_items[1], slot_items[2], slot_items[3], head_count, score_scale
            ),
            (slot_view(packed), lengths, log_sums, slot_view(dcontext)),
        )
        dpacked = dpacked.reshape(token_count, 3 * features).astype(jnp.bfloat16)
        dbias_in = jnp.sum(dpacked.astype(jnp.float32), axis=0)
        dinput = jnp.einsum("td,te->de", rounded, dpacked, preferred_element_type=jnp.float32)
        grad_main = dsum + jnp.einsum(
            "te,de->td", dpacked, in_full, preferred_element_type=jnp.float32
        )
        dvectors = jnp.concatenate(
            [
                dbias_in[:features],
                dbias_in[2 * features :],
                dbias_out,
                dgain_one,
                dshift_one,
                dbias_two,
                dgain_two,
                dshift_two,
                dbias_up,
            ]
        )
        layer_grads[layer_index] = (dinput, doutput, dexpand, dreduce, dvectors)
    stacked = [
        jnp.stack([layer_grads[layer_index][member] for layer_index in range(layer_count)])
        for member in range(5)
    ]
    summed = (
        lax.psum_scatter(stacked[0], ("wide", "narrow"), scatter_dimension=1, tiled=True),
        lax.psum_scatter(stacked[1], ("wide", "narrow"), scatter_dimension=1, tiled=True),
        lax.psum_scatter(stacked[2], ("wide", "narrow"), scatter_dimension=1, tiled=True),
        lax.psum_scatter(stacked[3], ("wide", "narrow"), scatter_dimension=1, tiled=True),
        lax.psum_scatter(stacked[4], ("wide", "narrow"), scatter_dimension=1, tiled=True),
        lax.psum_scatter(
            jnp.concatenate([grad_gain, grad_shift]),
            ("wide", "narrow"),
            scatter_dimension=0,
            tiled=True,
        ),
    )
    return (
        layer_out,
        grad_main,
        grad_side,
        summed[0],
        summed[1],
        summed[2],
        summed[3],
        summed[4],
        summed[5],
    )


def solution(mesh):
    placed = (
        P(("wide", "narrow"), None),
        P(("wide", "narrow"), None),
        P(("wide", "narrow"), None),
        P(("wide", "narrow"), None),
        P(None, ("wide", "narrow"), None),
        P(None, ("wide", "narrow"), None),
        P(None, ("wide", "narrow"), None),
        P(None, ("wide", "narrow"), None),
        P(None, ("wide", "narrow")),
        P(("wide", "narrow")),
    )
    return jax.shard_map(
        local,
        mesh=mesh,
        in_specs=placed,
        out_specs=(
            P(("wide", "narrow"), None),
            P(("wide", "narrow"), None),
            P(("wide", "narrow"), None),
            P(None, ("wide", "narrow"), None),
            P(None, ("wide", "narrow"), None),
            P(None, ("wide", "narrow"), None),
            P(None, ("wide", "narrow"), None),
            P(None, ("wide", "narrow")),
            P(("wide", "narrow")),
        ),
        check_vma=False,
    )
```

profile of v0, /device:TPU:0, one launch (start us, length us, event | category | flops | bytes accessed | tf_op | source)
XLA Modules:
  0.0 1364.5 jit_solution(9898177780543497744)
XLA Ops:
  13.9 43.5 %all-gather.8 = bf16[32,192,2]{1,2,0:T(2,128)(2,1)S(1)} all-gather(bf16[1,192,2]{1,2,0:T(2,128)(2,1)} %bitcast.818), channel_id=1, replica_groups=mesh['wide'=8,'narrow'=4] {'wide','narrow'}, dimensions={0}, use_global_device_ids=true | all-gather | bytes 25344 | tf_op jit(solution)/shard_map/all_gather | solution.py:144
  61.5 37.0 %all-reduce = bf16[1024]{0:T(1024)(128)(2,1)S(1)} all-reduce(bf16[1024]{0:T(1024)(128)(2,1)S(1)} %dynamic-update-slice), channel_id=1, replica_groups=mesh['wide'=8,'narrow'=4] {'wide','narrow'}, use_global_device_ids=true, to_apply=%add | all-reduce | flops 1024 | bytes 4096
  99.8 44.5 %all-gather.5 = bf16[1,512,512]{2,1,0:T(8,128)(2,1)} all-gather(bf16[1,16,512]{2,1,0:T(8,128)(2,1)S(1)} %get-tuple-element.1281), channel_id=7, replica_groups=mesh['wide'=8,'narrow'=4] {'wide','narrow'}, dimensions={1}, use_global_device_ids=true | all-gather | bytes 540672 | tf_op jit(solution)/shard_map/all_gather | solution.py:182
  144.4 41.5 %all-gather.1 = bf16[1,512,512]{2,1,0:T(8,128)(2,1)} all-gather(bf16[1,16,512]{2,1,0:T(8,128)(2,1)S(1)} %get-tuple-element.1282), channel_id=3, replica_groups=mesh['wide'=8,'narrow'=4] {'wide','narrow'}, dimensions={1}, use_global_device_ids=true | all-gather | bytes 540672 | tf_op jit(solution)/shard_map/all_gather | solution.py:182
  189.9 4.9 add_convert_fusion.1
  194.7 60.8 %conditional.8 = (f32[8,1024]{1,0:T(8,128)}, bf16[1024,512]{0,1:T(8,128)(2,1)}) conditional(s32[]{:T(128)} %bitcast.70, (bf16[1024,1536]{1,0:T(8,128)(2,1)}, s32[4]{0:T(128)S(1)}) %tuple.447, (bf16[1024,1536]{1,0:T(8,128)(2,1)}, s32[4]{0:T(128)S(1)}) %tuple.448), branch_computations={%region_0.5_spmd, %region_5.0_spmd} | conditional | flops 281018368 | bytes 36145420
  199.8 55.7 %while.124 = (s32[]{:T(128)}, bf16[8,1,1024,64]{2,3,1,0:T(8,128)(2,1)}, f32[8,1,1024]{2,0,1:T(8,128)}, bf16[8,1,1024,64]{2,3,0,1:T(8,128)(2,1)}, bf16[8,1,1024,6...) while((s32[]{:T(128)}, ...), condition=%wide.region_9.9_spmd.clone, body=%wide.region_6.8_spmd.clone.sunk | while | flops 281018368 | bytes 13285485 | solution.py:54
  260.5 7.4 fusion.192
  267.9 10.0 fusion.242
  278.2 5.5 add_convert_fusion
  283.7 60.9 %conditional.9 = (f32[8,1024]{1,0:T(8,128)}, bf16[1024,512]{0,1:T(8,128)(2,1)}) conditional(s32[]{:T(128)} %bitcast.70, (bf16[1024,1536]{1,0:T(8,128)(2,1)}, s32[4]{0:T(128)S(1)}) %tuple.449, (bf16[1024,1536]{1,0:T(8,128)(2,1)}, s32[4]{0:T(128)S(1)}) %tuple.450), branch_computations={%region_14.19_spmd, %region_19.24_spmd} | conditional | flops 281018368 | bytes 36145420
  288.9 55.7 %while.125 = (s32[]{:T(128)}, bf16[8,1,1024,64]{2,3,1,0:T(8,128)(2,1)}, f32[8,1,1024]{2,0,1:T(8,128)}, bf16[8,1,1024,64]{2,3,0,1:T(8,128)(2,1)}, bf16[8,1,1024,6...) while((s32[]{:T(128)}, ...), condition=%wide.region_23.23_spmd.clone, body=%wide.region_20.22_spmd.clone.sunk | while | flops 281018368 | bytes 13285485 | solution.py:54
  349.7 7.5 fusion.182
  361.6 10.8 fusion.239
  380.8 8.7 convert_reduce_fusion
  396.5 110.4 %conditional.20 = (bf16[1024,1536]{0,1:T(8,128)(2,1)}) conditional(s32[]{:T(128)} %bitcast.70, (bf16[1024,1536]{1,0:T(8,128)(2,1)}, f32[8,1024]{1,0:T(8,128)}, bf16[1024,512]{1,0:T(8,128)(2,1)S(1)}, s32[4]{0:T(128)S(1)}) %tuple.451, (bf16[1024,1536]{1,0:T(8,128)(2,1)}, f32[8,1024]{1,0:T(8,128)}, bf16[1024,512]{1,0:T(8,128)(2,1)S(1)}, ...), branch_computations={%region_36.40_spmd, %region_40.44_spmd} | conditional | flops 696385536 | bytes 61036860 | solution.py:120
  407.0 96.6 %while.127 = (s32[]{:T(128)}, bf16[8,1,1024,64]{2,3,1,0:T(8,128)(2,1)}, bf16[8,1,1024,64]{2,3,1,0:T(8,128)(2,1)}, bf16[8,1,1024,64]{2,3,1,0:T(8,128)(2,1)}, bf16...) while((s32[]{:T(128)}, ...), condition=%wide.region_43.43_spmd.clone, body=%wide.region_41.42_spmd.clone.sunk | while | flops 686948352 | bytes 33199228 | solution.py:82
  509.4 5.8 convolution_bitcast_fusion.4
  520.2 8.1 convert_reduce_fusion.1
  534.4 117.8 %conditional.21 = (bf16[1024,1536]{0,1:T(8,128)(2,1)}) conditional(s32[]{:T(128)} %bitcast.70, (bf16[1024,1536]{1,0:T(8,128)(2,1)}, f32[8,1024]{1,0:T(8,128)}, bf16[1024,512]{1,0:T(8,128)(2,1)S(1)}, s32[4]{0:T(128)S(1)}) %tuple.453, (bf16[1024,1536]{1,0:T(8,128)(2,1)}, f32[8,1024]{1,0:T(8,128)}, bf16[1024,512]{1,0:T(8,128)(2,1)S(1)}, ...), branch_computations={%region_48.52_spmd, %region_52.56_spmd} | conditional | flops 696385536 | bytes 61036860 | solution.py:120
  552.5 96.6 %while.129 = (s32[]{:T(128)}, bf16[8,1,1024,64]{2,3,1,0:T(8,128)(2,1)}, bf16[8,1,1024,64]{2,3,1,0:T(8,128)(2,1)}, bf16[8,1,1024,64]{2,3,1,0:T(8,128)(2,1)}, bf16...) while((s32[]{:T(128)}, ...), condition=%wide.region_55.55_spmd.clone, body=%wide.region_53.54_spmd.clone.sunk | while | flops 686948352 | bytes 33199228 | solution.py:82
  662.4 6.2 pad_maximum_fusion.6
  668.6 10.6 copy.251
  686.8 5.5 convolution_bitcast_fusion.8
  699.9 6.7 convolution_bitcast_fusion.6
  706.7 6.7 convolution_bitcast_fusion.7
  721.4 5.6 add_add_fusion.6
  730.0 38.7 %all-reduce.2 = f32[1024]{0:T(1024)S(1)} all-reduce(f32[1024]{0:T(1024)S(1)} %pad_maximum_fusion.11), channel_id=15, replica_groups=mesh['wide'=8,'narrow'=4] {'wide','narrow'}, use_global_device_ids=true, to_apply=%region_78.79.clone | all-reduce | flops 1024 | bytes 8192
  770.8 152.8 %all-reduce.5.cloned.1.call-done = f32[2,512,1536]{2,0,1:T(2,128)} async-done(((f32[2,512,1536]{2,0,1:T(2,128)}), f32[2,512,1536]{2,0,1:T(2,128)}) %all-reduce.5.cloned.1.call-update) | async-done | bytes 6291472
  925.3 137.3 %reduce-scatter.7.cloned.1.call-done = f32[2,16,512]{2,1,0:T(8,128)} async-done(((f32[2,512,512]{2,1,0:T(8,128)}), f32[2,16,512]{2,1,0:T(8,128)}) %reduce-scatter.7.cloned.1.call-update) | async-done | bytes 65552 | tf_op jit(solution)/shard_map/reduce_scatter | solution.py:282
  1062.6 147.6 %reduce-scatter.9.cloned.1.call-done = f32[2,16,2048]{2,1,0:T(8,128)} async-done(((f32[2,512,2048]{2,1,0:T(8,128)}), f32[2,16,2048]{2,1,0:T(8,128)}) %reduce-scatter.9.cloned.1.call-update) | async-done | bytes 262160 | tf_op jit(solution)/shard_map/reduce_scatter | solution.py:283
  1210.2 147.6 %reduce-scatter.11.cloned.1.call-done = f32[2,64,512]{2,1,0:T(8,128)} async-done(((f32[2,2048,512]{2,1,0:T(8,128)}), f32[2,64,512]{2,1,0:T(8,128)}) %reduce-scatter.11.cloned.1.call-update) | async-done | bytes 262160 | tf_op jit(solution)/shard_map/reduce_scatter | solution.py:284
  (534 shorter events, 439.3 us)
Async XLA Ops:
  7.2 178.7 %copy-start.23 = (bf16[1024,512]{1,0:T(8,128)(2,1)S(1)}, bf16[1024,512]{1,0:T(8,128)(2,1)}, u32[]{:S(2)}) copy-start(bf16[1024,512]{1,0:T(8,128)(2,1)} %param.36) | copy-start | bytes 3145732
  7.2 182.7 %all-gather.16.cloned.1.call-start = ((), (), s32[]{:S(2)}) async-start(), calls=%async_computation.7 | async-start | bytes 1622016 | tf_op jit(solution)/shard_map/all_gather | solution.py:181
  8.8 251.7 %all-gather.18.cloned.1.call-start = ((), (), s32[]{:S(2)}) async-start(), calls=%async_computation.8 | async-start | bytes 2162688 | tf_op jit(solution)/shard_map/all_gather | solution.py:196
  10.4 176.8 %copy-start.24 = (bf16[1024,512]{1,0:T(8,128)(2,1)S(1)}, bf16[1024,512]{1,0:T(8,128)(2,1)}, u32[]{:S(2)}) copy-start(bf16[1024,512]{1,0:T(8,128)(2,1)} %param.35) | copy-start | bytes 3145732
  10.4 257.5 %all-gather.20.cloned.1.call-start = ((), (), s32[]{:S(2)}) async-start(), calls=%async_computation.9 | async-start | bytes 2162688 | tf_op jit(solution)/shard_map/all_gather | solution.py:197
  12.1 266.1 %all-gather.22.cloned.1.call-start = ((), (), s32[]{:S(2)}) async-start(), calls=%async_computation.10 | async-start | bytes 1622016 | tf_op jit(solution)/shard_map/all_gather | solution.py:181
  12.7 336.7 %all-gather.24.cloned.1.call-start = ((), (), s32[]{:S(2)}) async-start(), calls=%async_computation.11 | async-start | bytes 2162688 | tf_op jit(solution)/shard_map/all_gather | solution.py:196
  13.2 348.4 %all-gather.26.cloned.1.call-start = ((), (), s32[]{:S(2)}) async-start(), calls=%async_computation.12 | async-start | bytes 2162688 | tf_op jit(solution)/shard_map/all_gather | solution.py:197
  13.8 755.4 %reduce-scatter.13.cloned.1.call-start = ((), (), s32[]{:S(2)}) async-start(), calls=%async_computation.13 | async-start | bytes 3244032
  58.1 209.7 %copy-start.65 = (f32[1,2048]{1,0:T(1,128)}, f32[1,2048]{1,0:T(1,128)S(1)}, u32[]{:S(2)}) copy-start(f32[1,2048]{1,0:T(1,128)S(1)} %get-tuple-element.1280) | copy-start | bytes 24580
  58.8 209.1 %copy-start.54 = (f32[1,512]{1,0:T(1,128)}, f32[1,512]{1,0:T(1,128)S(1)}, u32[]{:S(2)}) copy-start(f32[1,512]{1,0:T(1,128)S(1)} %get-tuple-element.1275) | copy-start | bytes 6148
  58.8 209.1 %copy-start.69 = (f32[1,512]{1,0:T(1,128)}, f32[1,512]{1,0:T(1,128)S(1)}, u32[]{:S(2)}) copy-start(f32[1,512]{1,0:T(1,128)S(1)} %get-tuple-element.1274) | copy-start | bytes 6148
  259.3 8.5 copy-start.5
  259.3 8.5 copy-start.41
  349.0 12.6 copy-start.1
  349.0 44.6 %copy-start.43 = (f32[1024]{0:T(1024)}, f32[1024]{0:T(1024)S(1)}, u32[]{:S(2)}) copy-start(f32[1024]{0:T(1024)S(1)} %broadcast_multiply_fusion.2) | copy-start | bytes 12292
  349.3 44.3 %copy-start.52 = (f32[1024]{0:T(1024)}, f32[1024]{0:T(1024)S(1)}, u32[]{:S(2)}) copy-start(f32[1024]{0:T(1024)S(1)} %fusion.222) | copy-start | bytes 12292
  349.7 12.0 copy-start.26
  349.7 12.0 copy-start.67
  349.7 12.0 copy-start.73
  361.6 10.9 copy-start
  361.6 10.9 copy-start.46
  372.5 8.3 slice-start.2
  380.8 8.7 copy-start.21
  380.8 8.7 copy-start.2
  380.8 8.7 copy-start.78
  509.4 9.3 slice-start
  518.7 9.7 copy-start.33
  662.4 261.3 %all-reduce.5.cloned.1.call-start = ((), (), s32[]{:S(2)}) async-start(), calls=%async_computation.14 | async-start | bytes 12582912
  679.3 383.4 %reduce-scatter.7.cloned.1.call-start = ((), (), s32[]{:S(2)}) async-start(), calls=%async_computation.4 | async-start | bytes 2162688 | tf_op jit(solution)/shard_map/reduce_scatter | solution.py:282
  686.1 524.1 %reduce-scatter.9.cloned.1.call-start = ((), (), s32[]{:S(2)}) async-start(), calls=%async_computation.5 | async-start | bytes 8650752 | tf_op jit(solution)/shard_map/reduce_scatter | solution.py:283
  698.7 659.1 %reduce-scatter.11.cloned.1.call-start = ((), (), s32[]{:S(2)}) async-start(), calls=%async_computation.6 | async-start | bytes 8650752 | tf_op jit(solution)/shard_map/reduce_scatter | solution.py:284
  (60 other events, 214.6 us)
Sparse Core Ops, SparseCore 0:
  11.5 57.6 all-gather.15
  72.6 56.1 all-gather.17
  132.2 55.8 all-gather.19
  190.8 53.6 all-gather.21
  247.8 55.2 all-gather.23
  306.4 55.1 all-gather.25
  662.5 100.5 reduce-scatter.12
  768.7 154.8 all-reduce.4
  926.6 136.0 reduce-scatter.6
  1065.3 144.7 reduce-scatter.8
  1213.1 144.6 reduce-scatter.10
where the time goes:
time: 1380 us; the launch traced here: 1360 us
  waiting for transfers between devices  592 us (43%)
  matrix products  363 us (26%)
  blocking collectives  205 us (15%)
  local copies, waits for them, and re-layouts  97.7 us (7%)
  other arithmetic  81.4 us (6%)
  between operations  15.8 us (1%)
    unnamed x13, waiting for transfers between devices  155 us
    reduce_scatter x1, waiting for transfers between devices, local(): lax.psum_scatter(stacked[3], ('wide', 'narrow'), scatter_dimension=1, til...  148 us
    reduce_scatter x1, waiting for transfers between devices, local(): lax.psum_scatter(stacked[2], ('wide', 'narrow'), scatter_dimension=1, til...  148 us
    reduce_scatter x1, waiting for transfers between devices, local(): lax.psum_scatter(stacked[1], ('wide', 'narrow'), scatter_dimension=1, til...  137 us
    all_gather x2, blocking collectives, local(): lax.all_gather(output_weight[layer_index], ('wide', 'narrow'), axis=0, ti...  86 us
    unnamed x2, blocking collectives  75.7 us
    dot_general x32, matrix products, masked_scores(): jnp.einsum('gqd,gkd->gqk', query_one, key_one, preferred_element_type=jnp...  54.8 us
    dot_general x16, matrix products, forward_one_head(): jnp.einsum('gqk,gkd->gqd', chances, value_one, preferred_element_type=jnp...  45.1 us
  transfers between devices with their start and end apart: 11, of which 5 were waited for; matrix products, arithmetic and copies ran while one was open for 18% of the time, Pallas kernels for 0%

commit v1 on v0

v1 whole, which is shorter than its diff:
```python
import functools

import jax
import jax.numpy as jnp
from jax import lax
from jax.experimental import pallas as pl
from jax.experimental.pallas import tpu as pltpu
from jax.sharding import PartitionSpec as P

HEAD_DIM = 64
AXES = ("wide", "narrow")
F32 = jnp.float32
BF16 = jnp.bfloat16
NN = (((1,), (0,)), ((), ()))
NT = (((1,), (1,)), ((), ()))
TN = (((0,), (0,)), ((), ()))
MASKED = -1000000000.0
VMEM_LIMIT = 60 * 2**20
BLOCK = 16
VMEM = pltpu.VMEM
ANY = pl.ANY


def mm(left, right, dims):
    return lax.dot_general(left, right, dims, preferred_element_type=F32)


def whole(memory=VMEM):
    return pl.BlockSpec(memory_space=memory)


def fixed(shape):
    zeros = (0,) * len(shape)
    return pl.BlockSpec(shape, lambda step: zeros)


def rows_of(tile, width):
    return pl.BlockSpec((tile, width), lambda step: (step, 0))


def each_slot(order_ref, stream, refs, act):
    for index, ref in enumerate(refs):
        count = ref.shape[0]

        def one(slot, carry, ref=ref, base=index * count):
            act(ref, slot, order_ref[stream, base + slot])
            return carry

        lax.fori_loop(0, count, one, 0)


def wait_all(ref, sem):
    pltpu.make_async_copy(ref, ref, sem).wait()


def fetch_attn(order_ref, alpha, beta, w_ref, sem):
    def fetch_qk(ref, slot, owner):
        pltpu.make_async_copy(ref.at[slot], w_ref.at[pl.ds(0, 2), owner], sem).start()

    def fetch_v(ref, slot, owner):
        pltpu.make_async_copy(ref.at[slot, 0], w_ref.at[2, owner], sem).start()

    each_slot(order_ref, 0, alpha, fetch_qk)
    each_slot(order_ref, 1, beta, fetch_v)


def attn_forward_body(
    order_ref,
    bounds_ref,
    x_ref,
    vec_ref,
    *refs,
):
    alpha, beta = refs[:4], refs[4:8]
    e_ref, qkv_ref, ctx_ref, rinv_ref, w_ref, aux_ref, rows_ref, sem = refs[8:]
    pair = pl.program_id(0)
    tokens, features = x_ref.shape
    lane = lax.broadcasted_iota(jnp.int32, (tokens, 128), 1)
    low_half = lane < HEAD_DIM

    @pl.when(pair == 0)
    def _():
        fetch_attn(order_ref, alpha, beta, w_ref, sem)
        token = lax.broadcasted_iota(jnp.int32, (tokens, 128), 0)
        column = lane % HEAD_DIM
        single = bounds_ref[0, 1] == 0
        quarter = tokens // 4
        segment = jnp.where(single, 0, token // quarter)
        inside = jnp.where(single, token, token % quarter)
        own = column == segment
        bound = jnp.where(
            segment == 0,
            bounds_ref[0, 0],
            jnp.where(
                segment == 1,
                bounds_ref[0, 1],
                jnp.where(segment == 2, bounds_ref[0, 2], bounds_ref[0, 3]),
            ),
        )
        alive = own & (inside < bound)
        aux_ref[0] = jnp.where(own, 1.0, 0.0).astype(BF16)
        aux_ref[1] = jnp.where(alive | (column >= 4), 0.0, MASKED).astype(BF16)
        wait_all(w_ref, sem)
        x = x_ref[...]
        for part in range(3):
            packed = mm(x, w_ref[part].reshape(features, features), NN)
            if part == 0:
                packed = (packed + vec_ref[0:1]).astype(BF16) * BF16(0.125)
            elif part == 2:
                packed = (packed + vec_ref[1:2]).astype(BF16)
            else:
                packed = packed.astype(BF16)
            for index in range(features // 128):
                qkv_ref[part, index] = packed[:, index * 128 : (index + 1) * 128]

    query = qkv_ref[0, pair]
    key = qkv_ref[1, pair]
    value_t = qkv_ref[2, pair].T
    ones = jnp.ones((16, tokens), BF16)
    chunk = 256
    outs = []
    for head in range(2):
        inside_head = low_half if head == 0 else ~low_half
        query_aug = jnp.where(inside_head, query, aux_ref[0])
        key_aug = jnp.where(inside_head, key, aux_ref[1])
        value_aug = jnp.concatenate(
            [value_t[head * HEAD_DIM : (head + 1) * HEAD_DIM], ones], axis=0
        )
        parts = []
        for start in range(0, tokens, chunk):
            scores = mm(key_aug, query_aug[start : start + chunk], NT)
            top = jnp.max(scores, axis=0, keepdims=True)
            exponent = jnp.exp(scores - top).astype(BF16)
            e_ref[head, :, start : start + chunk] = exponent
            mixed = mm(value_aug, exponent, NN)
            inverse = 1.0 / mixed[HEAD_DIM : HEAD_DIM + 1]
            rows_ref[pl.ds(pair * 2 + head, 1), start : start + chunk] = inverse
            parts.append(mixed[:HEAD_DIM] * inverse)
        outs.append(jnp.concatenate(parts, axis=1))
    ctx_ref[...] = jnp.concatenate(outs, axis=0).T.astype(BF16)

    @pl.when(pair == pl.num_programs(0) - 1)
    def _():
        rinv_ref[...] = jnp.concatenate(
            [rows_ref[...], jnp.zeros((120, tokens), F32)], axis=0
        ).T


def attn_forward(order, bounds, x, vec, weights):
    tokens, features = x.shape
    pairs = features // 128
    out_shape = (
        jax.ShapeDtypeStruct((2 * pairs, tokens, tokens), BF16),
        jax.ShapeDtypeStruct((3, pairs, tokens, 128), BF16),
        jax.ShapeDtypeStruct((tokens, features), BF16),
        jax.ShapeDtypeStruct((tokens, 128), F32),
    )
    return pl.pallas_call(
        attn_forward_body,
        grid=(pairs,),
        out_shape=out_shape,
        in_specs=[
            whole(pltpu.SMEM),
            whole(pltpu.SMEM),
            fixed(x.shape),
            fixed(vec.shape),
        ]
        + [whole(ANY)] * len(weights),
        out_specs=(
            pl.BlockSpec((2, tokens, tokens), lambda step: (step, 0, 0)),
            fixed((3, pairs, tokens, 128)),
            pl.BlockSpec((tokens, 128), lambda step: (0, step)),
            fixed((tokens, 128)),
        ),
        scratch_shapes=[
            VMEM((3, features // BLOCK, BLOCK, features), BF16),
            VMEM((2, tokens, 128), BF16),
            VMEM((2 * pairs, tokens), F32),
            pltpu.SemaphoreType.DMA,
        ],
        compiler_params=pltpu.CompilerParams(vmem_limit_bytes=VMEM_LIMIT),
        cost_estimate=pl.CostEstimate(
            flops=14 * 10**9, bytes_accessed=24 * 10**6, transcendentals=0
        ),
        name="attn_forward",
    )(order, bounds, x, vec, *weights)


def normed(z):
    centered = z - jnp.mean(z, axis=-1, keepdims=True)
    variance = jnp.mean(centered * centered, axis=-1, keepdims=True)
    rstd = lax.rsqrt(variance + 1e-05)
    return centered * rstd, rstd


def norm_back(grad, gain, xhat, rstd):
    scaled = grad * gain
    first = jnp.mean(scaled, axis=-1, keepdims=True)
    second = jnp.mean(scaled * xhat, axis=-1, keepdims=True)
    return rstd * (scaled - first - xhat * second)


GELU_A = 0.7978845608028654
GELU_B = 0.044715


def gelu_tanh(hidden):
    square = hidden * hidden
    return jnp.tanh(hidden * (GELU_A + (GELU_A * GELU_B) * square)), square


def gelu(hidden):
    tanh, _ = gelu_tanh(hidden)
    half = 0.5 * hidden
    return half + half * tanh


def gelu_both(hidden):
    tanh, square = gelu_tanh(hidden)
    half = 0.5 * hidden
    cdf = 0.5 + 0.5 * tanh
    slope = GELU_A + (3.0 * GELU_A * GELU_B) * square
    return hidden * cdf, cdf + half * (1.0 - tanh * tanh) * slope


def column_sum(ref, row, values):
    ref[row : row + 1] += jnp.sum(values.astype(F32), axis=0, keepdims=True)


def ffn_body(forward, backward, last, *refs):
    refs = list(refs)
    take = lambda: refs.pop(0)
    order_ref, vec_ref = take(), take()
    alpha, beta = [take() for _ in range(4)], [take() for _ in range(4)]
    ctx_ref = take()
    if forward:
        x_ref, y_ref = take(), take()
    else:
        xh1_ref, xh2_ref, stat_ref, m1b_ref, hid_ref, gm_ref, gs_ref = [take() for _ in range(7)]
    if last:
        cot_ref = take()
    if backward:
        rinv_ref = take()
    if forward and not backward:
        xh1_out, xh2_out, stat_out, m1b_out, hid_out, m2_out, m2b_out, y_out = [
            take() for _ in range(8)
        ]
    if last:
        layer_out, gs_out = take(), take()
    if backward:
        dz1_out, do_out, dvec_out = [take() for _ in range(3)]
        galpha, gbeta = [take() for _ in range(2)], [take() for _ in range(2)]
    wo_ref, up_ref, down_ref, sem_o, sem_u, sem_d = [take() for _ in range(6)]
    if backward:
        act_s, dhid_s, m1b_s, df_s, da_s, ctx_s, gup_s, gdown_s, go_s = [
            take() for _ in range(9)
        ]
    assert not refs
    step = pl.program_id(0)
    tile, features = ctx_ref.shape
    groups = up_ref.shape[0]
    wo = lambda: wo_ref[...].reshape(features, features)
    up = lambda j: up_ref[j].reshape(features, features)
    per = features // BLOCK
    down = lambda j: down_ref[j * per : (j + 1) * per].reshape(features, features)

    @pl.when(step == 0)
    def _():
        def fetch_out(ref, slot, owner):
            pltpu.make_async_copy(ref.at[slot, groups], wo_ref.at[owner], sem_o).start()

        def fetch_up(ref, slot, owner):
            pltpu.make_async_copy(
                ref.at[slot, pl.ds(0, groups)], up_ref.at[:, owner], sem_u
            ).start()

        def fetch_down(ref, slot, owner):
            pltpu.make_async_copy(
                ref.at[slot], down_ref.at[pl.ds(owner * groups, groups)], sem_d
            ).start()

        each_slot(order_ref, 0, alpha, fetch_out)
        each_slot(order_ref, 0, alpha, fetch_up)
        each_slot(order_ref, 1, beta, fetch_down)
        if backward:
            dvec_out[...] = jnp.zeros_like(dvec_out)
        wait_all(wo_ref, sem_o)
        wait_all(up_ref, sem_u)
        wait_all(down_ref, sem_d)

    vec = lambda row: vec_ref[row : row + 1]
    ctx = ctx_ref[...]
    if forward:
        branch = mm(ctx, wo(), NN) + vec(2)
        xh1, rstd1 = normed(x_ref[...].astype(F32) + branch)
        m1 = xh1 * vec(3) + vec(4)
        y = y_ref[...].astype(F32) + branch
        m1b = m1.astype(BF16)
        hidden = [mm(m1b, up(j), NN) + vec(8 + j) for j in range(groups)]
        if backward:
            both = [gelu_both(h) for h in hidden]
            act = [pair[0].astype(BF16) for pair in both]
        else:
            act = [gelu(h).astype(BF16) for h in hidden]
        branch = vec(5)
        for j in range(groups):
            branch = branch + mm(act[j], down(j), NN)
        xh2, rstd2 = normed(m1 + branch)
        m2 = xh2 * vec(6) + vec(7)
        y = y + branch
        if not backward:
            xh1_out[...] = xh1.astype(BF16)
            xh2_out[...] = xh2.astype(BF16)
            stat_out[...] = jnp.where(
                lax.broadcasted_iota(jnp.int32, (tile, 128), 1) < 64, rstd1, rstd2
            )
            m1b_out[...] = m1b
            for j in range(groups):
                hid_out[:, j * features : (j + 1) * features] = hidden[j].astype(BF16)
            m2_out[...] = m2
            m2b_out[...] = m2.astype(BF16)
            y_out[...] = y
    else:
        xh1 = xh1_ref[...].astype(F32)
        xh2 = xh2_ref[...].astype(F32)
        stat = stat_ref[...]
        rstd1, rstd2 = stat[:, 0:1], stat[:, 64:65]
        m1b = m1b_ref[...]
        both = [
            gelu_both(hid_ref[:, j * features : (j + 1) * features].astype(F32))
            for j in range(groups)
        ]
        act = [pair[0].astype(BF16) for pair in both]
    if last:
        yh, rstdy = normed(y)
        layer_out[...] = (m2 + yh * vec(12) + vec(13)).astype(BF16)
        gm = cot_ref[...].astype(F32)
        gs = norm_back(gm, vec(12), yh, rstdy)
        gs_out[...] = gs
        column_sum(dvec_out, 12, gm * yh)
        column_sum(dvec_out, 13, gm)
    elif backward:
        gm = gm_ref[...]
        gs = gs_ref[...]
    if not backward:
        return
    rows = pl.ds(pl.multiple_of(step * tile, tile), tile)
    column_sum(dvec_out, 6, gm * xh2)
    column_sum(dvec_out, 7, gm)
    dz2 = norm_back(gm, vec(6), xh2, rstd2)
    df = (dz2 + gs).astype(BF16)
    column_sum(dvec_out, 5, df)
    df_s[rows] = df
    m1b_s[rows] = m1b
    ctx_s[rows] = ctx
    gm = dz2
    for j in range(groups):
        columns = slice(j * features, (j + 1) * features)
        dhid = (both[j][1] * mm(df, down(j), NT)).astype(BF16)
        column_sum(dvec_out, 8 + j, dhid)
        dhid_s[rows, columns] = dhid
        act_s[rows, columns] = act[j]
        gm = gm + mm(dhid, up(j), NT)
    column_sum(dvec_out, 3, gm * xh1)
    column_sum(dvec_out, 4, gm)
    dz1 = norm_back(gm, vec(3), xh1, rstd1)
    dz1_out[...] = dz1
    da = (dz1 + gs).astype(BF16)
    column_sum(dvec_out, 2, da)
    da_s[rows] = da
    dctx = mm(da, wo(), NT)
    lane = lax.broadcasted_iota(jnp.int32, (tile, 128), 1)
    low_half = lane < HEAD_DIM
    column = lane % HEAD_DIM
    for pair in range(features // 128):
        columns = slice(pair * 128, (pair + 1) * 128)
        dpair = dctx[:, columns]
        product = dpair * ctx[:, columns].astype(F32)
        for head in range(2):
            inside = low_half if head == 0 else ~low_half
            inverse = rinv_ref[:, 2 * pair + head : 2 * pair + head + 1]
            dot = -inverse * jnp.sum(jnp.where(inside, product, 0.0), axis=-1, keepdims=True)
            high = dot.astype(BF16).astype(F32)
            extra = jnp.where(column == 0, high, jnp.where(column == 1, dot - high, 0.0))
            do_out[2 * pair + head] = jnp.where(inside, dpair * inverse, extra).astype(BF16)

    @pl.when(step == pl.num_programs(0) - 1)
    def _():
        shape = (per, BLOCK, features)
        for j in range(groups):
            columns = slice(j * features, (j + 1) * features)
            gdown_s[j * per : (j + 1) * per] = (
                mm(act_s[:, columns], df_s[...], TN).astype(BF16).reshape(shape)
            )
            gup_s[j] = mm(m1b_s[...], dhid_s[:, columns], TN).astype(BF16).reshape(shape)
        go_s[...] = mm(ctx_s[...], da_s[...], TN).astype(BF16).reshape(shape)

        def send_alpha(ref, slot, owner):
            pltpu.make_async_copy(
                gup_s.at[:, owner], ref.at[slot, pl.ds(0, groups)], sem_u
            ).start()
            pltpu.make_async_copy(go_s.at[owner], ref.at[slot, groups], sem_o).start()

        def send_beta(ref, slot, owner):
            pltpu.make_async_copy(
                gdown_s.at[pl.ds(owner * groups, groups)], ref.at[slot], sem_d
            ).start()

        each_slot(order_ref, 0, galpha, send_alpha)
        each_slot(order_ref, 1, gbeta, send_beta)
        wait_all(gup_s, sem_u)
        wait_all(go_s, sem_o)
        wait_all(gdown_s, sem_d)


def ffn_call(forward, backward, last, order, vec, weights, ctx, tiled, rinv):
    tokens, features = ctx.shape
    tile = 256
    groups = 4
    width = groups * features
    per = features // BLOCK
    shapes = []
    if forward and not backward:
        shapes += [
            ((tokens, features), BF16),
            ((tokens, features), BF16),
            ((tokens, 128), F32),
            ((tokens, features), BF16),
            ((tokens, width), BF16),
            ((tokens, features), F32),
            ((tokens, features), BF16),
            ((tokens, features), F32),
        ]
    if last:
        shapes += [((tokens, features), BF16), ((tokens, features), F32)]
    out_specs = [rows_of(tile, shape[1]) for shape, _ in shapes]
    if backward:
        heads = features // HEAD_DIM
        shapes += [((tokens, features), F32), ((heads, tokens, 128), BF16), ((16, features), F32)]
        shapes += [((per // 2, groups + 1, BLOCK, features), BF16)] * 2
        shapes += [((per // 2, groups, BLOCK, features), BF16)] * 2
        out_specs += [
            rows_of(tile, features),
            pl.BlockSpec((heads, tile, 128), lambda step: (0, step, 0)),
            fixed((16, features)),
        ] + [whole(ANY)] * 4
    scratch = [
        VMEM((per, BLOCK, features), BF16),
        VMEM((groups, per, BLOCK, features), BF16),
        VMEM((groups * per, BLOCK, features), BF16),
        pltpu.SemaphoreType.DMA,
        pltpu.SemaphoreType.DMA,
        pltpu.SemaphoreType.DMA,
    ]
    if backward:
        scratch += [
            VMEM((tokens, width), BF16),
            VMEM((tokens, width), BF16),
            VMEM((tokens, features), BF16),
            VMEM((tokens, features), BF16),
            VMEM((tokens, features), BF16),
            VMEM((tokens, features), BF16),
            VMEM((groups, per, BLOCK, features), BF16),
            VMEM((groups * per, BLOCK, features), BF16),
            VMEM((per, BLOCK, features), BF16),
        ]
    operands = [ctx] + list(tiled) + ([rinv] if backward else [])
    return pl.pallas_call(
        functools.partial(ffn_body, forward, backward, last),
        grid=(tokens // tile,),
        out_shape=tuple(jax.ShapeDtypeStruct(shape, dtype) for shape, dtype in shapes),
        in_specs=[whole(pltpu.SMEM), fixed(vec.shape)]
        + [whole(ANY)] * len(weights)
        + [rows_of(tile, operand.shape[1]) for operand in operands],
        out_specs=tuple(out_specs),
        scratch_shapes=scratch,
        compiler_params=pltpu.CompilerParams(vmem_limit_bytes=VMEM_LIMIT),
        cost_estimate=pl.CostEstimate(
            flops=(6 * forward + 12 * backward) * 10**9, bytes_accessed=16 * 10**6, transcendentals=0
        ),
        name="ffn_" + ("f" if forward else "") + ("b" if backward else ""),
    )(order, vec, *weights, *operands)


def attn_backward_body(
    order_ref,
    e_ref,
    do_ref,
    qkv_ref,
    x_ref,
    dz_ref,
    *refs,
):
    alpha, beta = refs[:4], refs[4:8]
    gm_out, dvec_out = refs[8:10]
    galpha, gbeta = refs[10:12], refs[12:14]
    w_ref, dqkv_s, ds_s, g_s, sem, sem_a, sem_b = refs[14:]
    pair = pl.program_id(0)
    tokens, features = x_ref.shape
    lane = lax.broadcasted_iota(jnp.int32, (tokens, 128), 1)
    low_half = lane < HEAD_DIM
    column = lane % HEAD_DIM

    @pl.when(pair == 0)
    def _():
        fetch_attn(order_ref, alpha, beta, w_ref, sem)

    query = qkv_ref[0, 0]
    key_t = qkv_ref[1, 0].T
    value = qkv_ref[2, 0]
    ones = jnp.where(column < 2, 1.0, 0.0).astype(BF16)
    chunk = 256
    dquery, dkey, dvalue = [], [], []
    for head in range(2):
        inside = low_half if head == 0 else ~low_half
        value_aug = jnp.where(inside, value, ones)
        key_head = key_t[head * HEAD_DIM : (head + 1) * HEAD_DIM]
        parts = []
        for start in range(0, tokens, chunk):
            columns = slice(start, start + chunk)
            dchances = mm(value_aug, do_ref[head, columns], NT)
            dscores = (e_ref[head, :, columns].astype(F32) * dchances).astype(BF16)
            ds_s[head, :, columns] = dscores
            parts.append(mm(key_head, dscores, NN))
        dquery.append(jnp.concatenate(parts, axis=1))
        dkey.append(mm(ds_s[head], query, NN))
        dvalue.append(mm(e_ref[head], do_ref[head], NN))
    here = pl.ds(pl.multiple_of(pair * 128, 128), 128)
    dqkv_s[0, :, here] = (jnp.concatenate(dquery, axis=0).T * 0.125).astype(BF16)
    dqkv_s[1, :, here] = jnp.where(low_half, dkey[0], dkey[1]).astype(BF16)
    dqkv_s[2, :, here] = jnp.where(low_half, dvalue[0], dvalue[1]).astype(BF16)

    @pl.when(pair == pl.num_programs(0) - 1)
    def _():
        wait_all(w_ref, sem)
        x = x_ref[...]
        per = features // BLOCK
        for part in range(3):
            g_s[part] = (
                mm(x, dqkv_s[part], TN).astype(BF16).reshape((per, BLOCK, features))
            )

        def send_alpha(ref, slot, owner):
            pltpu.make_async_copy(g_s.at[pl.ds(0, 2), owner], ref.at[slot], sem_a).start()

        def send_beta(ref, slot, owner):
            pltpu.make_async_copy(g_s.at[2, owner], ref.at[slot, 0], sem_b).start()

        each_slot(order_ref, 0, galpha, send_alpha)
        each_slot(order_ref, 1, gbeta, send_beta)
        gm = dz_ref[...]
        for part in range(3):
            gm = gm + mm(dqkv_s[part], w_ref[part].reshape(features, features), NT)
        gm_out[...] = gm
        dvec_out[...] = jnp.zeros_like(dvec_out)
        column_sum(dvec_out, 0, dqkv_s[0])
        column_sum(dvec_out, 1, dqkv_s[2])
        wait_all(g_s.at[pl.ds(0, 2)], sem_a)
        wait_all(g_s.at[2], sem_b)


def attn_backward(order, e, do, qkv, x, dz, weights):
    tokens, features = x.shape
    pairs = features // 128
    per = features // BLOCK
    return pl.pallas_call(
        attn_backward_body,
        grid=(pairs,),
        out_shape=(
            jax.ShapeDtypeStruct((tokens, features), F32),
            jax.ShapeDtypeStruct((8, features), F32),
        )
        + (jax.ShapeDtypeStruct((per // 2, 2, BLOCK, features), BF16),) * 2
        + (jax.ShapeDtypeStruct((per // 2, 1, BLOCK, features), BF16),) * 2,
        in_specs=[
            whole(pltpu.SMEM),
            pl.BlockSpec((2, tokens, tokens), lambda step: (step, 0, 0)),
            pl.BlockSpec((2, tokens, 128), lambda step: (step, 0, 0)),
            pl.BlockSpec((3, 1, tokens, 128), lambda step: (0, step, 0, 0)),
            fixed(x.shape),
            fixed(dz.shape),
        ]
        + [whole(ANY)] * len(weights),
        out_specs=(fixed(dz.shape), fixed((8, features))) + (whole(ANY),) * 4,
        scratch_shapes=[
            VMEM((3, per, BLOCK, features), BF16),
            VMEM((3, tokens, features), BF16),
            VMEM((2, tokens, tokens), BF16),
            VMEM((3, per, BLOCK, features), BF16),
            pltpu.SemaphoreType.DMA,
            pltpu.SemaphoreType.DMA,
            pltpu.SemaphoreType.DMA,
        ],
        compiler_params=pltpu.CompilerParams(vmem_limit_bytes=VMEM_LIMIT),
        cost_estimate=pl.CostEstimate(
            flops=26 * 10**9, bytes_accessed=24 * 10**6, transcendentals=0
        ),
        name="attn_backward",
    )(order, e, do, qkv, x, dz, *weights)


def blocks_of(matrix, features):
    rows, columns = matrix.shape
    shaped = matrix.reshape(rows // BLOCK, BLOCK, columns // features, features)
    return shaped.transpose(0, 2, 1, 3)


def matrix_of(blocks):
    rows, columns, block, features = blocks.shape
    return blocks.transpose(0, 2, 1, 3).reshape(rows * block, columns * features)


CORE, X, Y, Z = 1, 2, 4, 8
Z_MASKS = (0, Z, 2 * Z, 3 * Z)


def slot_masks(first, second):
    return [
        core | high | low | z
        for core in (0, CORE)
        for high in (0, second)
        for low in (0, first)
        for z in Z_MASKS
    ]


def swap(part, mask):
    return lax.ppermute(part, AXES, [(device, device ^ mask) for device in range(32)])


def gather_streams(alpha, beta):
    cut = alpha.shape[0]
    own = jnp.concatenate([alpha, beta])
    pieces = [own] + [swap(own, mask) for mask in Z_MASKS[1:]]
    alpha4 = jnp.stack([piece[:cut] for piece in pieces])
    beta4 = jnp.stack([piece[cut:] for piece in pieces])
    alpha8 = jnp.concatenate([alpha4, swap(alpha4, Y)])
    beta8 = jnp.concatenate([beta4, swap(beta4, X)])
    alpha16 = [alpha8, swap(alpha8, X)]
    beta16 = [beta8, swap(beta8, Y)]
    return (
        alpha16 + [swap(part, CORE) for part in alpha16],
        beta16 + [swap(part, CORE) for part in beta16],
    )


def add(left, right):
    return (left.astype(F32) + right.astype(F32)).astype(BF16)


def scatter_streams(alpha, beta):
    totals = []
    cut = alpha[0].shape[1]
    stages = []
    for (mine, other), first, second in ((alpha, Y, X), (beta, X, Y)):
        stages.append((mine, swap(other, CORE), first, second))
    for mine, got, first, second in stages:
        half = mine.shape[0] // 2
        mine, sent = add(mine[:half], got[:half]), add(mine[half:], got[half:])
        got = swap(sent, second)
        half = half // 2
        mine, sent = add(mine[:half], got[:half]), add(mine[half:], got[half:])
        totals.append(add(mine, swap(sent, first)))
    joined = jnp.concatenate(totals, axis=1)
    total = joined[0].astype(F32)
    for index in range(1, 4):
        total = total + swap(joined[index], Z_MASKS[index]).astype(F32)
    return total[:cut], total[cut:]


def local(
    main_residual,
    side_residual,
    cotangent,
    lengths,
    input_weight,
    output_weight,
    expand_weight,
    reduce_weight,
    vectors,
    final_norm,
):
    tokens, features = main_residual.shape
    layers = input_weight.shape[0]
    assert lengths.shape[0] == 1 and layers == 2
    per = features // BLOCK
    groups = expand_weight.shape[2] // features
    fast = lax.axis_size(AXES) == 32 and per == 32

    if fast:
        me = lax.axis_index(AXES)
        order = jnp.stack(
            [
                me ^ jnp.array(slot_masks(Y, X), jnp.int32),
                me ^ jnp.array(slot_masks(X, Y), jnp.int32),
            ]
        )
        width = vectors.shape[1]
        spread = final_norm.shape[0]
        row = jnp.concatenate([vectors[0], vectors[1], final_norm])
        row = jnp.pad(row[None], ((0, BLOCK - 1), (0, features - row.shape[0])))
        attn_w, ffn_w = [], []
        for layer in range(layers):
            qkv = blocks_of(input_weight[layer], features)[0]
            beta = qkv[2:]
            if layer == 0:
                beta = jnp.concatenate([beta, row[None]])
            attn_w.append(gather_streams(qkv[:2], beta))
            ffn_w.append(
                gather_streams(
                    jnp.concatenate(
                        [blocks_of(expand_weight[layer], features)[0], output_weight[layer][None]]
                    ),
                    reduce_weight[layer].reshape(groups, BLOCK, features),
                )
            )
        rows = jnp.concatenate([part[:, 1, 0] for part in attn_w[0][1]])
        rows = jnp.zeros_like(rows).at[order[1]].set(rows, unique_indices=True)
        all_vectors = jnp.stack(
            [rows[:, layer * width : (layer + 1) * width].reshape(-1) for layer in range(layers)]
        ).astype(F32)
        final_full = rows[:, layers * width : layers * width + spread].reshape(-1).astype(F32)
    else:
        gather = lambda part, axis: lax.all_gather(part, AXES, axis=axis, tiled=True)
        order = jnp.tile(jnp.arange(per, dtype=jnp.int32)[None], (2, 1))
        quarters = lambda blocks: [blocks[index * 8 : index * 8 + 8] for index in range(4)]
        all_vectors = gather(vectors, 1).astype(F32)
        final_full = gather(final_norm, 0).astype(F32)
        attn_w, ffn_w = [], []
        for layer in range(layers):
            qkv = blocks_of(gather(input_weight[layer], 0), features)
            attn_w.append((quarters(qkv[:, :2]), quarters(qkv[:, 2:])))
            up = blocks_of(gather(expand_weight[layer], 0), features)
            out = blocks_of(gather(output_weight[layer], 0), features)
            down = gather(reduce_weight[layer], 0).reshape(per, -1, BLOCK, features)
            ffn_w.append((quarters(jnp.concatenate([up, out], axis=1)), quarters(down)))
    attn_w = [alpha + beta for alpha, beta in attn_w]
    ffn_w = [alpha + beta for alpha, beta in ffn_w]
    vec = jnp.concatenate(
        [
            all_vectors.reshape(layers, 12, features),
            jnp.broadcast_to(final_full.reshape(1, 2, features), (layers, 2, features)),
            jnp.zeros((layers, 2, features), F32),
        ],
        axis=1,
    )

    e0, qkv0, ctx0, rinv0 = attn_forward(order, lengths, main_residual, vec[0], attn_w[0])
    xh1, xh2, stat, m1b, hid, m2, m2b, y = ffn_call(
        True, False, False, order, vec[0], ffn_w[0], ctx0, (main_residual, side_residual), None
    )
    e1, qkv1, ctx1, rinv1 = attn_forward(order, lengths, m2b, vec[1], attn_w[1])
    layer_out, grad_side, dz, do, dvec1, *gf1 = ffn_call(
        True, True, True, order, vec[1], ffn_w[1], ctx1, (m2, y, cotangent), rinv1
    )
    gm, dvec1a, *gi1 = attn_backward(order, e1, do, qkv1, m2b, dz, attn_w[1])
    dz, do, dvec0, *gf0 = ffn_call(
        False, True, False, order, vec[0], ffn_w[0], ctx0,
        (xh1, xh2, stat, m1b, hid, gm, grad_side), rinv0,
    )
    grad_main, dvec0a, *gi0 = attn_backward(order, e0, do, qkv0, main_residual, dz, attn_w[0])

    dvec = jnp.stack(
        [
            jnp.concatenate([dvec0a[0:2], dvec0[2:12]]).reshape(-1),
            jnp.concatenate([dvec1a[0:2], dvec1[2:12]]).reshape(-1),
        ]
    )
    dfinal = dvec1[12:14].reshape(-1)
    if fast:
        up1, down1 = scatter_streams(gf1[:2], gf1[2:])
        in1 = scatter_streams(gi1[:2], gi1[2:])
        up0, down0 = scatter_streams(gf0[:2], gf0[2:])
        rows = jnp.concatenate(
            [
                dvec.reshape(layers, per, width).transpose(1, 0, 2).reshape(per, -1),
                dfinal.reshape(per, spread),
            ],
            axis=1,
        )[order[1]].astype(BF16)
        rows = jnp.pad(
            rows[:, None, None],
            ((0, 0), (0, 0), (0, BLOCK - 1), (0, features - rows.shape[1])),
        )
        half = per // 2
        alpha0, beta0 = scatter_streams(
            gi0[:2],
            [
                jnp.concatenate([gi0[2], rows[:half]], axis=1),
                jnp.concatenate([gi0[3], rows[half:]], axis=1),
            ],
        )
        grad_vec = beta0[1, 0, : layers * width].reshape(layers, width)
        grad_final = beta0[1, 0, layers * width : layers * width + spread]
        side = lambda blocks: blocks.transpose(1, 0, 2).reshape(BLOCK, -1)
        grad_in = jnp.stack(
            [side(jnp.concatenate([alpha0, beta0[:1]])), side(jnp.concatenate(in1))]
        )
        grad_out = jnp.stack([up0[groups], up1[groups]])
        grad_up = jnp.stack([side(up0[:groups]), side(up1[:groups])])
        grad_down = jnp.stack([down0.reshape(-1, features), down1.reshape(-1, features)])
    else:
        scatter = lambda part, axis: lax.psum_scatter(
            part, AXES, scatter_dimension=axis, tiled=True
        ).astype(F32)
        both = lambda make: jnp.stack([make(*gi0, *gf0), make(*gi1, *gf1)])
        join = lambda left, right: jnp.concatenate([left, right])
        grad_in = scatter(
            both(
                lambda a0, a1, b0, b1, *_: matrix_of(
                    jnp.concatenate([join(a0, a1), join(b0, b1)], axis=1)
                )
            ),
            1,
        )
        grad_out = scatter(
            both(lambda *g: matrix_of(join(g[4], g[5])[:, groups:])), 1
        )
        grad_up = scatter(both(lambda *g: matrix_of(join(g[4], g[5])[:, :groups])), 1)
        grad_down = scatter(both(lambda *g: join(g[6], g[7]).reshape(-1, features)), 1)
        grad_vec = scatter(dvec, 1)
        grad_final = scatter(dfinal, 0)
    return (
        layer_out,
        grad_main,
        grad_side,
        grad_in,
        grad_out,
        grad_up,
        grad_down,
        grad_vec,
        grad_final,
    )


def solution(mesh):
    rows = P(AXES, None)
    middle = P(None, AXES, None)
    return jax.shard_map(
        local,
        mesh=mesh,
        in_specs=(rows, rows, rows, rows, middle, middle, middle, middle, P(None, AXES), P(AXES)),
        out_specs=(rows, rows, rows, middle, middle, middle, middle, P(None, AXES), P(AXES)),
        check_vma=False,
    )
```

time: 1380 us -> 443 us (0.32)
  waiting for transfers between devices: 592 us -> 114 us
  matrix products: 363 us -> 0 us
  Pallas kernels: 0 us -> 210 us
  blocking collectives: 205 us -> 0 us
  starting transfers between devices: 0.66 us -> 83.7 us
  local copies, waits for them, and re-layouts: 97.7 us -> 15.3 us
  other arithmetic: 81.4 us -> 12.6 us
    reduce_scatter x3 -> x0, waiting for transfers between devices: 432 us -> none  [the longest x1 148 us: local(): lax.psum_scatter(stacked[3], ('wide', 'narrow'), scatter_dimension=1, til...]
    dot_general x136 -> x0, matrix products: 363 us -> none  [the longest x32 54.8 us: masked_scores(): jnp.einsum('gqd,gkd->gqk', query_one, key_one, preferred_element_type=jnp...]
    pallas_call x0 -> x7, Pallas kernels: none -> 210 us  [the longest x3 76.4 us: ffn_call(): pl.pallas_call(functools.partial(ffn_body, forward, backward, last), grid...]
    unnamed x13 -> x0, waiting for transfers between devices: 155 us -> none
    all_gather x3 -> x0, blocking collectives: 130 us -> none  [the longest x2 86 us: local(): lax.all_gather(output_weight[layer_index], ('wide', 'narrow'), axis=0, ti...]
    ppermute x0 -> x80, waiting for transfers between devices: none -> 114 us  [swap(): lax.ppermute(part, AXES, [(device, device ^ mask) for device in range(32)])]
    ppermute x0 -> x80, starting transfers between devices: none -> 83.7 us  [swap(): lax.ppermute(part, AXES, [(device, device ^ mask) for device in range(32)])]
    unnamed x2 -> x0, blocking collectives: 75.7 us -> none
  transfers between devices with their start and end apart: 11 -> 80, of which waited for: 5 -> 28; matrix products, arithmetic and copies ran while one was open for 18% -> 4% of each run, Pallas kernels for 0% -> 18%
where the time goes in v1:
time: 443 us; the launch traced here: 438 us
  Pallas kernels  210 us (47%)
  waiting for transfers between devices  114 us (26%)
  starting transfers between devices  83.7 us (19%)
  local copies, waits for them, and re-layouts  15.3 us (3%)
  other arithmetic  12.6 us (3%)
    ppermute x80, waiting for transfers between devices, swap(): lax.ppermute(part, AXES, [(device, device ^ mask) for device in range(32)])  114 us
    ppermute x80, starting transfers between devices, swap(): lax.ppermute(part, AXES, [(device, device ^ mask) for device in range(32)])  83.7 us
    pallas_call x3, Pallas kernels, ffn_call(): pl.pallas_call(functools.partial(ffn_body, forward, backward, last), grid...  76.4 us
    pallas_call x2, Pallas kernels, attn_backward(): pl.pallas_call(attn_backward_body, grid=(pairs,), out_shape=(jax.ShapeDty...  67.3 us
    pallas_call x2, Pallas kernels, attn_forward(): pl.pallas_call(attn_forward_body, grid=(pairs,), out_shape=out_shape, in_...  66.4 us
  transfers between devices with their start and end apart: 80, of which 28 were waited for; matrix products, arithmetic and copies ran while one was open for 4% of the time, Pallas kernels for 18%

profile of v1, /device:TPU:0, one launch (start us, length us, event | category | flops | bytes accessed | tf_op | source)
XLA Modules:
  0.0 438.5 jit_solution(14294797514990975202)
XLA Ops:
  3.1 3.1 collective-permute-start
  6.2 2.6 collective-permute-start.1
  9.7 3.0 collective-permute-start.35
  18.5 3.1 collective-permute-done.34
  28.2 2.7 collective-permute-done.40
  30.8 2.5 collective-permute-start.8
  33.4 3.3 collective-permute-done.19
  36.7 2.3 collective-permute-start.9
  53.6 3.7 collective-permute-done.25
  65.5 4.5 %collective-permute-done.10 = bf16[4,5,16,512]{3,2,1,0:T(8,128)(2,1)S(1)} collective-permute-done((bf16[4,5,16,512]{3,2,1,0:T(8,128)(2,1)S(1)}, bf16[4,5,16,512]{3,2,1,0:T(8,128)(2,1)S(1)}, u32[]{:S(2)}, u32[]{:S(2)}) %collective-permute-start.10) | collective-permute-done | bytes 327712 | tf_op jit(solution)/shard_map/ppermute | solution.py:628
  76.5 15.5 %collective-permute-done.37.refs_1_ = bf16[8,2,16,512]{3,2,1,0:T(8,128)(2,1)} collective-permute-done((bf16[8,2,16,512]{3,2,1,0:T(8,128)(2,1)}, bf16[8,2,16,512]{3,2,1,0:T(8,128)(2,1)}, u32[]{:S(2)}, u32[]{:S(2)}) %collective-permute-start.37) | collective-permute-done | bytes 262176 | tf_op jit(solution)/shard_map/ppermute | solution.py:628
  94.5 33.1 %attn_forward.2 = (bf16[8,1024,1024]{2,1,0:T(8,128)(2,1)}, bf16[3,4,1024,128]{3,2,1,0:T(8,128)(2,1)}, bf16[1024,512]{1,0:T(8,128)(2,1)}, f32[1024,128]{1,0:T(8,128)}) custom-call(s32[2,32]{1,0:T(2,128)} %pad_add_fusion.order_ref.refs_0_, s32[1,4]{1,0:T(1,128)} %bounds_ref.3, bf16[1024,512]{1,0:T(8,128)(2,1)} %x_ref.3, ...), custom_call_target="tpu_custom_call" | custom-call | flops 14000000000 | bytes 24000000 | tf_op jit(solution)/shard_map/attn_forward/pallas_call | solution.py:158
  129.8 13.1 %ffn_f.1 = (bf16[1024,512]{1,0:T(8,128)(2,1)}, bf16[1024,512]{1,0:T(8,128)(2,1)}, f32[1024,128]{1,0:T(8,128)}, bf16[1024,512]{1,0:T(8,128)(2,1)}, bf16[1024,2048...) custom-call(s32[2,32]{1,0:T(2,128)} %pad_add_fusion.order_ref.refs_0_, ...), custom_call_target="tpu_custom_call" | custom-call | flops 6000000000 | bytes 16000000 | tf_op jit(solution)/shard_map/ffn_f/pallas_call | solution.py:468
  144.9 33.2 %attn_forward.3 = (bf16[8,1024,1024]{2,1,0:T(8,128)(2,1)}, bf16[3,4,1024,128]{3,2,1,0:T(8,128)(2,1)}, bf16[1024,512]{1,0:T(8,128)(2,1)}, f32[1024,128]{1,0:T(8,128)}) custom-call(s32[2,32]{1,0:T(2,128)} %pad_add_fusion.order_ref.refs_0_, s32[1,4]{1,0:T(1,128)} %bounds_ref.3, bf16[1024,512]{1,0:T(8,128)(2,1)} %get-tuple-element.54.x_ref, ...), custom_call_target="tpu_custom_call" | custom-call | flops 14000000000 | bytes 24000000 | tf_op jit(solution)/shard_map/attn_forward/pallas_call | solution.py:158
  179.4 34.1 %ffn_fb.1 = (bf16[1024,512]{1,0:T(8,128)(2,1)}, f32[1024,512]{1,0:T(8,128)}, f32[1024,512]{1,0:T(8,128)}, bf16[8,1024,128]{2,1,0:T(8,128)(2,1)}, f32[16,512]{1,0...) custom-call(s32[2,32]{1,0:T(2,128)} %pad_add_fusion.order_ref.refs_0, ...), custom_call_target="tpu_custom_call" | custom-call | flops 17999998976 | bytes 16000000 | tf_op jit(solution)/shard_map/ffn_fb/pallas_call | solution.py:468
  213.5 33.7 %attn_backward.2 = (f32[1024,512]{1,0:T(8,128)}, f32[8,512]{1,0:T(8,128)}, bf16[16,2,16,512]{3,2,1,0:T(8,128)(2,1)}, bf16[16,2,16,512]{3,2,1,0:T(8,128)(2,1)}, b...) custom-call(s32[2,32]{1,0:T(2,128)} %pad_add_fusion.order_ref.refs_0_, ...), custom_call_target="tpu_custom_call" | custom-call | flops 25999998976 | bytes 24000000 | tf_op jit(solution)/shard_map/attn_backward/pallas_call | solution.py:566
  247.2 29.2 %ffn_b.1 = (f32[1024,512]{1,0:T(8,128)}, bf16[8,1024,128]{2,1,0:T(8,128)(2,1)}, f32[16,512]{1,0:T(8,128)}, bf16[16,5,16,512]{3,2,1,0:T(8,128)(2,1)}, bf16[16,5,1...) custom-call(s32[2,32]{1,0:T(2,128)} %pad_add_fusion.order_ref.refs_0_, ...), custom_call_target="tpu_custom_call" | custom-call | flops 12000000000 | bytes 16000000 | tf_op jit(solution)/shard_map/ffn_b/pallas_call | solution.py:468
  276.4 33.6 %attn_backward.3 = (f32[1024,512]{1,0:T(8,128)}, f32[8,512]{1,0:T(8,128)}, bf16[16,2,16,512]{3,2,1,0:T(8,128)(2,1)}, bf16[16,2,16,512]{3,2,1,0:T(8,128)(2,1)}, b...) custom-call(s32[2,32]{1,0:T(2,128)} %pad_add_fusion.order_ref.refs_0_, ...), custom_call_target="tpu_custom_call" | custom-call | flops 25999998976 | bytes 24000000 | tf_op jit(solution)/shard_map/attn_backward/pallas_call | solution.py:566
  314.3 5.0 %collective-permute-done.57 = bf16[8,1,16,512]{3,2,1,0:T(8,128)(2,1)S(1)} collective-permute-done((bf16[8,1,16,512]{3,2,1,0:T(8,128)(2,1)S(1)}, bf16[8,1,16,512]{3,2,1,0:T(8,128)(2,1)S(1)}, u32[]{:S(2)}, u32[]{:S(2)}) %collective-permute-start.57) | collective-permute-done | bytes 131104 | tf_op jit(solution)/shard_map/ppermute | solution.py:628
  320.4 3.2 collective-permute-done.58
  327.3 5.3 %collective-permute-done.48 = bf16[8,2,16,512]{3,2,1,0:T(8,128)(2,1)S(1)} collective-permute-done((bf16[8,2,16,512]{3,2,1,0:T(8,128)(2,1)S(1)}, bf16[8,2,16,512]{3,2,1,0:T(8,128)(2,1)S(1)}, u32[]{:S(2)}, u32[]{:S(2)}) %collective-permute-start.48) | collective-permute-done | bytes 262176 | tf_op jit(solution)/shard_map/ppermute | solution.py:628
  335.5 4.0 collective-permute-done.45
  341.2 5.7 %collective-permute-start.59 = (bf16[3,16,512]{2,1,0:T(8,128)(2,1)S(1)}, bf16[3,16,512]{2,1,0:T(8,128)(2,1)S(1)}, u32[]{:S(2)}, u32[]{:S(2)}) collective-permute-start(bf16[3,16,512]{2,1,0:T(8,128)(2,1)S(1)} %get-tuple-element.128), channel_id=1, source_target_pairs={{0,8},{1,9},{2,10},{3,11},{4,12},{5,13},{6,14},{7,15},{8,0},{9,1},... | collective-permute-start | bytes 147464 | tf_op jit(solution)/shard_map/ppermute | solution.py:628
  347.4 2.3 collective-permute-start.61
  353.5 2.7 collective-permute-start.52
  368.8 9.9 %collective-permute-done.66 = bf16[8,4,16,512]{3,2,1,0:T(8,128)(2,1)S(1)} collective-permute-done((bf16[8,4,16,512]{3,2,1,0:T(8,128)(2,1)S(1)}, bf16[8,4,16,512]{3,2,1,0:T(8,128)(2,1)S(1)}, u32[]{:S(2)}, u32[]{:S(2)}) %collective-permute-start.66) | collective-permute-done | bytes 524320 | tf_op jit(solution)/shard_map/ppermute | solution.py:628
  381.5 6.5 %collective-permute-done.75 = bf16[8,4,16,512]{3,2,1,0:T(8,128)(2,1)S(1)} collective-permute-done((bf16[8,4,16,512]{3,2,1,0:T(8,128)(2,1)S(1)}, bf16[8,4,16,512]{3,2,1,0:T(8,128)(2,1)S(1)}, u32[]{:S(2)}, u32[]{:S(2)}) %collective-permute-start.75) | collective-permute-done | bytes 524320 | tf_op jit(solution)/shard_map/ppermute | solution.py:628
  388.7 2.9 collective-permute-done.67
  393.4 15.3 %collective-permute-done.76 = bf16[4,4,16,512]{3,2,1,0:T(8,128)(2,1)S(1)} collective-permute-done((bf16[4,4,16,512]{3,2,1,0:T(8,128)(2,1)S(1)}, bf16[4,4,16,512]{3,2,1,0:T(8,128)(2,1)S(1)}, u32[]{:S(2)}, u32[]{:S(2)}) %collective-permute-start.76) | collective-permute-done | bytes 262176 | tf_op jit(solution)/shard_map/ppermute | solution.py:628
  416.5 2.3 collective-permute-start.78
  421.6 3.4 collective-permute-done.69
  425.2 10.4 %collective-permute-done.78 = bf16[9,16,512]{2,1,0:T(8,128)(2,1)S(1)} collective-permute-done((bf16[9,16,512]{2,1,0:T(8,128)(2,1)S(1)}, bf16[9,16,512]{2,1,0:T(8,128)(2,1)S(1)}, u32[]{:S(2)}, u32[]{:S(2)}) %collective-permute-start.78) | collective-permute-done | bytes 147488 | tf_op jit(solution)/shard_map/ppermute | solution.py:628
  (390 shorter events, 100.6 us)
Async XLA Ops:
  3.1 21.4 %collective-permute-start = (bf16[4,16,512]{2,1,0:T(8,128)(2,1)S(1)}, bf16[4,16,512]{2,1,0:T(8,128)(2,1)S(1)}, u32[]{:S(2)}, u32[]{:S(2)}) collective-permute-start(bf16[4,16,512]{2,1,0:T(8,128)(2,1)S(1)} %pad_maximum_fusion.17), channel_id=1, source_target_pairs={{0,8},{1,9},{2,10},{3,11},{4,12},{5,13},{6,14},{7,15},{8,0},{9,1},... | collective-permute-start | bytes 196616 | tf_op jit(solution)/shard_map/ppermute | solution.py:628
  6.2 20.1 %collective-permute-start.1 = (bf16[4,16,512]{2,1,0:T(8,128)(2,1)S(1)}, bf16[4,16,512]{2,1,0:T(8,128)(2,1)S(1)}, u32[]{:S(2)}, u32[]{:S(2)}) collective-permute-start(bf16[4,16,512]{2,1,0:T(8,128)(2,1)S(1)} %pad_maximum_fusion.17), channel_id=1, source_target_pairs={{0,16},{1,17},{2,18},{3,19},{4,20},{5,21},{6,22},{7,23},{8,24},{9,... | collective-permute-start | bytes 196616 | tf_op jit(solution)/shard_map/ppermute | solution.py:628
  8.8 17.7 %collective-permute-start.2 = (bf16[4,16,512]{2,1,0:T(8,128)(2,1)S(1)}, bf16[4,16,512]{2,1,0:T(8,128)(2,1)S(1)}, u32[]{:S(2)}, u32[]{:S(2)}) collective-permute-start(bf16[4,16,512]{2,1,0:T(8,128)(2,1)S(1)} %pad_maximum_fusion.17), channel_id=1, source_target_pairs={{0,24},{1,25},{2,26},{3,27},{4,28},{5,29},{6,30},{7,31},{8,16},{9,... | collective-permute-start | bytes 196616 | tf_op jit(solution)/shard_map/ppermute | solution.py:628
  21.6 17.5 %collective-permute-start.18 = (bf16[9,16,512]{2,1,0:T(8,128)(2,1)S(1)}, bf16[9,16,512]{2,1,0:T(8,128)(2,1)S(1)}, u32[]{:S(2)}, u32[]{:S(2)}) collective-permute-start(bf16[9,16,512]{2,1,0:T(8,128)(2,1)S(1)} %pad_maximum_fusion.12), channel_id=1, source_target_pairs={{0,8},{1,9},{2,10},{3,11},{4,12},{5,13},{6,14},{7,15},{8,0},{9,1},... | collective-permute-start | bytes 442376 | tf_op jit(solution)/shard_map/ppermute | solution.py:628
  24.5 16.2 %collective-permute-start.20 = (bf16[9,16,512]{2,1,0:T(8,128)(2,1)S(1)}, bf16[9,16,512]{2,1,0:T(8,128)(2,1)S(1)}, u32[]{:S(2)}, u32[]{:S(2)}) collective-permute-start(bf16[9,16,512]{2,1,0:T(8,128)(2,1)S(1)} %pad_maximum_fusion.12), channel_id=1, source_target_pairs={{0,24},{1,25},{2,26},{3,27},{4,28},{5,29},{6,30},{7,31},{8,16},{9,... | collective-permute-start | bytes 442376 | tf_op jit(solution)/shard_map/ppermute | solution.py:628
  26.3 22.2 %collective-permute-start.7 = (bf16[9,16,512]{2,1,0:T(8,128)(2,1)S(1)}, bf16[9,16,512]{2,1,0:T(8,128)(2,1)S(1)}, u32[]{:S(2)}, u32[]{:S(2)}) collective-permute-start(bf16[9,16,512]{2,1,0:T(8,128)(2,1)S(1)} %pad_maximum_fusion.11), channel_id=1, source_target_pairs={{0,8},{1,9},{2,10},{3,11},{4,12},{5,13},{6,14},{7,15},{8,0},{9,1},... | collective-permute-start | bytes 442376 | tf_op jit(solution)/shard_map/ppermute | solution.py:628
  30.8 16.1 %collective-permute-start.8 = (bf16[9,16,512]{2,1,0:T(8,128)(2,1)S(1)}, bf16[9,16,512]{2,1,0:T(8,128)(2,1)S(1)}, u32[]{:S(2)}, u32[]{:S(2)}) collective-permute-start(bf16[9,16,512]{2,1,0:T(8,128)(2,1)S(1)} %pad_maximum_fusion.11), channel_id=1, source_target_pairs={{0,16},{1,17},{2,18},{3,19},{4,20},{5,21},{6,22},{7,23},{8,24},{9,... | collective-permute-start | bytes 442376 | tf_op jit(solution)/shard_map/ppermute | solution.py:628
  46.9 17.0 %collective-permute-start.21 = (bf16[4,5,16,512]{3,2,1,0:T(8,128)(2,1)S(1)}, bf16[4,5,16,512]{3,2,1,0:T(8,128)(2,1)S(1)}, u32[]{:S(2)}, u32[]{:S(2)}) collective-permute-start(bf16[4,5,16,512]{3,2,1,0:T(8,128)(2,1)S(1)} %pad_maximum_fusion.2), channel_id=1, source_target_pairs={{0,4},{1,5},{2,6},{3,7},{4,0},{5,1},{6,2},{7,3},{8,12},{9,13},{10,... | collective-permute-start | bytes 983048 | tf_op jit(solution)/shard_map/ppermute | solution.py:628
  70.0 23.9 %collective-permute-start.26 = (bf16[8,4,16,512]{3,2,1,0:T(8,128)(2,1)}, bf16[8,4,16,512]{3,2,1,0:T(8,128)(2,1)}, u32[]{:S(2)}, u32[]{:S(2)}) collective-permute-start(bf16[8,4,16,512]{3,2,1,0:T(8,128)(2,1)} %constant_dynamic-update-slice_fusion.20.refs_6_), channel_id=1, source_target_pairs={{0,4},{1,5},{2,6},{3,7},{4,0},{5,1},{6,2},{7,3},{8,12},{9,13},{10,... | collective-permute-start | bytes 1572872 | tf_op jit(solution)/shard_map/ppermute | solution.py:628
  71.6 22.4 %collective-permute-start.22 = (bf16[8,5,16,512]{3,2,1,0:T(8,128)(2,1)S(1)}, bf16[8,5,16,512]{3,2,1,0:T(8,128)(2,1)}, u32[]{:S(2)}, u32[]{:S(2)}) collective-permute-start(bf16[8,5,16,512]{3,2,1,0:T(8,128)(2,1)S(1)} %constant_dynamic-update-slice_fusion.15.refs_2_), channel_id=1, source_target_pairs={{0,2},{1,3},{2,0},{3,1},{4,6},{5,7},{6,4},{7,5},{8,10},{9,11},{10,... | collective-permute-start | bytes 1966088 | tf_op jit(solution)/shard_map/ppermute | solution.py:628
  74.5 17.4 %collective-permute-start.37 = (bf16[8,2,16,512]{3,2,1,0:T(8,128)(2,1)}, bf16[8,2,16,512]{3,2,1,0:T(8,128)(2,1)}, u32[]{:S(2)}, u32[]{:S(2)}) collective-permute-start(bf16[8,2,16,512]{3,2,1,0:T(8,128)(2,1)} %copy-done.17), channel_id=1, source_target_pairs={{0,2},{1,3},{2,0},{3,1},{4,6},{5,7},{6,4},{7,5},{8,10},{9,11},{10,... | collective-permute-start | bytes 786440 | tf_op jit(solution)/shard_map/ppermute | solution.py:628
  75.3 16.7 %collective-permute-start.31 = (bf16[8,2,16,512]{3,2,1,0:T(8,128)(2,1)S(1)}, bf16[8,2,16,512]{3,2,1,0:T(8,128)(2,1)S(1)}, u32[]{:S(2)}, u32[]{:S(2)}) collective-permute-start(bf16[8,2,16,512]{3,2,1,0:T(8,128)(2,1)S(1)} %constant_dynamic-update-slice_fusion.25.refs_0_), channel_id=1, source_target_pairs={{0,1},{1,0},{2,3},{3,2},{4,5},{5,4},{6,7},{7,6},{8,9},{9,8},{10,11... | collective-permute-start | bytes 786440 | tf_op jit(solution)/shard_map/ppermute | solution.py:628
  75.3 17.2 %collective-permute-start.32 = (bf16[8,2,16,512]{3,2,1,0:T(8,128)(2,1)}, bf16[8,2,16,512]{3,2,1,0:T(8,128)(2,1)S(1)}, u32[]{:S(2)}, u32[]{:S(2)}) collective-permute-start(bf16[8,2,16,512]{3,2,1,0:T(8,128)(2,1)} %collective-permute-done.30.refs_1_), channel_id=1, source_target_pairs={{0,1},{1,0},{2,3},{3,2},{4,5},{5,4},{6,7},{7,6},{8,9},{9,8},{10,11... | collective-permute-start | bytes 786440 | tf_op jit(solution)/shard_map/ppermute | solution.py:628
  92.0 35.7 %collective-permute-start.27 = (bf16[8,4,16,512]{3,2,1,0:T(8,128)(2,1)}, bf16[8,4,16,512]{3,2,1,0:T(8,128)(2,1)S(1)}, u32[]{:S(2)}, u32[]{:S(2)}) collective-permute-start(bf16[8,4,16,512]{3,2,1,0:T(8,128)(2,1)} %constant_dynamic-update-slice_fusion.20.refs_6_), channel_id=1, source_target_pairs={{0,1},{1,0},{2,3},{3,2},{4,5},{5,4},{6,7},{7,6},{8,9},{9,8},{10,11... | collective-permute-start | bytes 1572872 | tf_op jit(solution)/shard_map/ppermute | solution.py:628
  92.0 35.9 %collective-permute-start.23 = (bf16[8,5,16,512]{3,2,1,0:T(8,128)(2,1)S(1)}, bf16[8,5,16,512]{3,2,1,0:T(8,128)(2,1)S(1)}, u32[]{:S(2)}, u32[]{:S(2)}) collective-permute-start(bf16[8,5,16,512]{3,2,1,0:T(8,128)(2,1)S(1)} %constant_dynamic-update-slice_fusion.15.refs_2_), channel_id=1, source_target_pairs={{0,1},{1,0},{2,3},{3,2},{4,5},{5,4},{6,7},{7,6},{8,9},{9,8},{10,11... | collective-permute-start | bytes 1966088 | tf_op jit(solution)/shard_map/ppermute | solution.py:628
  92.5 51.6 %collective-permute-start.11 = (bf16[8,5,16,512]{3,2,1,0:T(8,128)(2,1)S(1)}, bf16[8,5,16,512]{3,2,1,0:T(8,128)(2,1)}, u32[]{:S(2)}, u32[]{:S(2)}) collective-permute-start(bf16[8,5,16,512]{3,2,1,0:T(8,128)(2,1)S(1)} %constant_dynamic-update-slice_fusion.5.refs_2_), channel_id=1, source_target_pairs={{0,2},{1,3},{2,0},{3,1},{4,6},{5,7},{6,4},{7,5},{8,10},{9,11},{10,... | collective-permute-start | bytes 1966088 | tf_op jit(solution)/shard_map/ppermute | solution.py:628
  94.0 34.3 %collective-permute-start.28 = (bf16[8,4,16,512]{3,2,1,0:T(8,128)(2,1)}, bf16[8,4,16,512]{3,2,1,0:T(8,128)(2,1)}, u32[]{:S(2)}, u32[]{:S(2)}) collective-permute-start(bf16[8,4,16,512]{3,2,1,0:T(8,128)(2,1)} %collective-permute-done.26.refs_7_), channel_id=1, source_target_pairs={{0,1},{1,0},{2,3},{3,2},{4,5},{5,4},{6,7},{7,6},{8,9},{9,8},{10,11... | collective-permute-start | bytes 1572872 | tf_op jit(solution)/shard_map/ppermute | solution.py:628
  94.0 35.8 %collective-permute-start.24 = (bf16[8,5,16,512]{3,2,1,0:T(8,128)(2,1)}, bf16[8,5,16,512]{3,2,1,0:T(8,128)(2,1)}, u32[]{:S(2)}, u32[]{:S(2)}) collective-permute-start(bf16[8,5,16,512]{3,2,1,0:T(8,128)(2,1)} %collective-permute-done.22.refs_3_), channel_id=1, source_target_pairs={{0,1},{1,0},{2,3},{3,2},{4,5},{5,4},{6,7},{7,6},{8,9},{9,8},{10,11... | collective-permute-start | bytes 1966088 | tf_op jit(solution)/shard_map/ppermute | solution.py:628
  143.0 35.2 %collective-permute-start.16 = (bf16[8,4,16,512]{3,2,1,0:T(8,128)(2,1)S(1)}, bf16[8,4,16,512]{3,2,1,0:T(8,128)(2,1)S(1)}, u32[]{:S(2)}, u32[]{:S(2)}) collective-permute-start(bf16[8,4,16,512]{3,2,1,0:T(8,128)(2,1)S(1)} %constant_dynamic-update-slice_fusion.10.refs_6_), channel_id=1, source_target_pairs={{0,1},{1,0},{2,3},{3,2},{4,5},{5,4},{6,7},{7,6},{8,9},{9,8},{10,11... | collective-permute-start | bytes 1572872 | tf_op jit(solution)/shard_map/ppermute | solution.py:628
  143.5 34.6 %collective-permute-start.12 = (bf16[8,5,16,512]{3,2,1,0:T(8,128)(2,1)S(1)}, bf16[8,5,16,512]{3,2,1,0:T(8,128)(2,1)S(1)}, u32[]{:S(2)}, u32[]{:S(2)}) collective-permute-start(bf16[8,5,16,512]{3,2,1,0:T(8,128)(2,1)S(1)} %constant_dynamic-update-slice_fusion.5.refs_2_), channel_id=1, source_target_pairs={{0,1},{1,0},{2,3},{3,2},{4,5},{5,4},{6,7},{7,6},{8,9},{9,8},{10,11... | collective-permute-start | bytes 1966088 | tf_op jit(solution)/shard_map/ppermute | solution.py:628
  143.6 34.6 %collective-permute-start.17 = (bf16[8,4,16,512]{3,2,1,0:T(8,128)(2,1)}, bf16[8,4,16,512]{3,2,1,0:T(8,128)(2,1)}, u32[]{:S(2)}, u32[]{:S(2)}) collective-permute-start(bf16[8,4,16,512]{3,2,1,0:T(8,128)(2,1)} %collective-permute-done.15.refs_7_), channel_id=1, source_target_pairs={{0,1},{1,0},{2,3},{3,2},{4,5},{5,4},{6,7},{7,6},{8,9},{9,8},{10,11... | collective-permute-start | bytes 1572872 | tf_op jit(solution)/shard_map/ppermute | solution.py:628
  144.1 34.1 %collective-permute-start.13 = (bf16[8,5,16,512]{3,2,1,0:T(8,128)(2,1)}, bf16[8,5,16,512]{3,2,1,0:T(8,128)(2,1)S(1)}, u32[]{:S(2)}, u32[]{:S(2)}) collective-permute-start(bf16[8,5,16,512]{3,2,1,0:T(8,128)(2,1)} %collective-permute-done.11.refs_3_), channel_id=1, source_target_pairs={{0,1},{1,0},{2,3},{3,2},{4,5},{5,4},{6,7},{7,6},{8,9},{9,8},{10,11... | collective-permute-start | bytes 1966088 | tf_op jit(solution)/shard_map/ppermute | solution.py:628
  319.9 41.9 %collective-permute-start.65 = (bf16[16,4,16,512]{3,2,1,0:T(8,128)(2,1)}, bf16[16,4,16,512]{3,2,1,0:T(8,128)(2,1)}, u32[]{:S(2)}, u32[]{:S(2)}) collective-permute-start(bf16[16,4,16,512]{3,2,1,0:T(8,128)(2,1)} %get-tuple-element.92), channel_id=1, source_target_pairs={{0,1},{1,0},{2,3},{3,2},{4,5},{5,4},{6,7},{7,6},{8,9},{9,8},{10,11... | collective-permute-start | bytes 3145736 | tf_op jit(solution)/shard_map/ppermute | solution.py:628
  320.4 47.3 %collective-permute-start.62 = (bf16[16,5,16,512]{3,2,1,0:T(8,128)(2,1)}, bf16[16,5,16,512]{3,2,1,0:T(8,128)(2,1)S(1)}, u32[]{:S(2)}, u32[]{:S(2)}) collective-permute-start(bf16[16,5,16,512]{3,2,1,0:T(8,128)(2,1)} %get-tuple-element.90), channel_id=1, source_target_pairs={{0,1},{1,0},{2,3},{3,2},{4,5},{5,4},{6,7},{7,6},{8,9},{9,8},{10,11... | collective-permute-start | bytes 3932168 | tf_op jit(solution)/shard_map/ppermute | solution.py:628
  358.2 21.2 %collective-permute-start.71 = (bf16[16,5,16,512]{3,2,1,0:T(8,128)(2,1)}, bf16[16,5,16,512]{3,2,1,0:T(8,128)(2,1)S(1)}, u32[]{:S(2)}, u32[]{:S(2)}) collective-permute-start(bf16[16,5,16,512]{3,2,1,0:T(8,128)(2,1)} %get-tuple-element.94), channel_id=1, source_target_pairs={{0,1},{1,0},{2,3},{3,2},{4,5},{5,4},{6,7},{7,6},{8,9},{9,8},{10,11... | collective-permute-start | bytes 3932168 | tf_op jit(solution)/shard_map/ppermute | solution.py:628
  367.1 20.9 %collective-permute-start.75 = (bf16[8,4,16,512]{3,2,1,0:T(8,128)(2,1)S(1)}, bf16[8,4,16,512]{3,2,1,0:T(8,128)(2,1)S(1)}, u32[]{:S(2)}, u32[]{:S(2)}) collective-permute-start(bf16[8,4,16,512]{3,2,1,0:T(8,128)(2,1)S(1)} %get-tuple-element.106), channel_id=1, source_target_pairs={{0,4},{1,5},{2,6},{3,7},{4,0},{5,1},{6,2},{7,3},{8,12},{9,13},{10,... | collective-permute-start | bytes 1572872 | tf_op jit(solution)/shard_map/ppermute | solution.py:628
  368.2 23.5 %collective-permute-start.63 = (bf16[8,5,16,512]{3,2,1,0:T(8,128)(2,1)S(1)}, bf16[8,5,16,512]{3,2,1,0:T(8,128)(2,1)S(1)}, u32[]{:S(2)}, u32[]{:S(2)}) collective-permute-start(bf16[8,5,16,512]{3,2,1,0:T(8,128)(2,1)S(1)} %get-tuple-element.100), channel_id=1, source_target_pairs={{0,2},{1,3},{2,0},{3,1},{4,6},{5,7},{6,4},{7,5},{8,10},{9,11},{10,... | collective-permute-start | bytes 1966088 | tf_op jit(solution)/shard_map/ppermute | solution.py:628
  380.0 28.9 %collective-permute-start.72 = (bf16[8,5,16,512]{3,2,1,0:T(8,128)(2,1)S(1)}, bf16[8,5,16,512]{3,2,1,0:T(8,128)(2,1)S(1)}, u32[]{:S(2)}, u32[]{:S(2)}) collective-permute-start(bf16[8,5,16,512]{3,2,1,0:T(8,128)(2,1)S(1)} %get-tuple-element.102), channel_id=1, source_target_pairs={{0,2},{1,3},{2,0},{3,1},{4,6},{5,7},{6,4},{7,5},{8,10},{9,11},{10,... | collective-permute-start | bytes 1966088 | tf_op jit(solution)/shard_map/ppermute | solution.py:628
  388.1 20.7 %collective-permute-start.76 = (bf16[4,4,16,512]{3,2,1,0:T(8,128)(2,1)S(1)}, bf16[4,4,16,512]{3,2,1,0:T(8,128)(2,1)S(1)}, u32[]{:S(2)}, u32[]{:S(2)}) collective-permute-start(bf16[4,4,16,512]{3,2,1,0:T(8,128)(2,1)S(1)} %add_convert_fusion.15), channel_id=1, source_target_pairs={{0,2},{1,3},{2,0},{3,1},{4,6},{5,7},{6,4},{7,5},{8,10},{9,11},{10,... | collective-permute-start | bytes 786440 | tf_op jit(solution)/shard_map/ppermute | solution.py:628
  391.8 18.8 %collective-permute-start.64 = (bf16[4,5,16,512]{3,2,1,0:T(8,128)(2,1)S(1)}, bf16[4,5,16,512]{3,2,1,0:T(8,128)(2,1)S(1)}, u32[]{:S(2)}, u32[]{:S(2)}) collective-permute-start(bf16[4,5,16,512]{3,2,1,0:T(8,128)(2,1)S(1)} %add_convert_fusion.12), channel_id=1, source_target_pairs={{0,4},{1,5},{2,6},{3,7},{4,0},{5,1},{6,2},{7,3},{8,12},{9,13},{10,... | collective-permute-start | bytes 983048 | tf_op jit(solution)/shard_map/ppermute | solution.py:628
  416.5 19.0 %collective-permute-start.78 = (bf16[9,16,512]{2,1,0:T(8,128)(2,1)S(1)}, bf16[9,16,512]{2,1,0:T(8,128)(2,1)S(1)}, u32[]{:S(2)}, u32[]{:S(2)}) collective-permute-start(bf16[9,16,512]{2,1,0:T(8,128)(2,1)S(1)} %get-tuple-element.118), channel_id=1, source_target_pairs={{0,16},{1,17},{2,18},{3,19},{4,20},{5,21},{6,22},{7,23},{8,24},{9,... | collective-permute-start | bytes 442376 | tf_op jit(solution)/shard_map/ppermute | solution.py:628
  419.3 16.2 %collective-permute-start.79 = (bf16[9,16,512]{2,1,0:T(8,128)(2,1)S(1)}, bf16[9,16,512]{2,1,0:T(8,128)(2,1)S(1)}, u32[]{:S(2)}, u32[]{:S(2)}) collective-permute-start(bf16[9,16,512]{2,1,0:T(8,128)(2,1)S(1)} %get-tuple-element.117), channel_id=1, source_target_pairs={{0,24},{1,25},{2,26},{3,27},{4,28},{5,29},{6,30},{7,31},{8,16},{9,... | collective-permute-start | bytes 442376 | tf_op jit(solution)/shard_map/ppermute | solution.py:628
  (87 other events, 1112.5 us)
